TPU v7x, 128 devices: a whole 4x4x4 slice. The times are simulated.
128 devices in a mesh: seq: 32 (over y, z, core), head: 4 (over x).
Axes of the slice: x: 4, y: 4, z: 4, core: 2. Of those that a mesh axis runs over, the one named last changes fastest.
Arguments:
- x_input: bfloat16 [32768, 8192], P('seq', 'head'), may hold values from -6 to 6
- z_input: bfloat16 [32768, 8192], P('seq', 'head'), may hold values from -6 to 6
- bc_input: bfloat16 [32768, 8, 256], P('seq', 'head'), may hold values from -6 to 6
- conv_weight_x: float32 [4, 8192], P(None, 'head'), may hold values from -3 to 3
- conv_weight_bc: float32 [4, 8, 256], P(None, 'head'), may hold values from -3 to 3
- step_size: float32 [32768, 128], P('seq', 'head'), may hold values from 0 to 1
- log_decay: float32 [32768, 128], P('seq', 'head'), may hold values from -1 to 0
- skip_gain: float32 [128], P('head'), may hold values from 0.5 to 2
- norm_gain: float32 [8192], P('head'), may hold values from 0.1 to 1.9
- out_weight: bfloat16 [8192, 4096], P('head'), may hold values from -0.0625 to 0.0625
Outputs:
- layer_out: bfloat16 [32768, 4096], P(('seq', 'head'))
All inputs are finite; a program needn't handle non-finite values.
Results may differ from a plain program's by a relative error of at most 0.012.
Values may be sent and summed in bfloat16 or wider, within the bound.
A program may use at most 256 MiB of HBM per device.

v0:
```python
import jax
import jax.numpy as jnp
from jax import lax
from jax.sharding import PartitionSpec as P

P_SIZE = 64
N = 128
KCONV = 4
BLOCK_LEN = 256


EPS = 1e-05


def from_behind(block, axis, distance):
    devices = range(lax.axis_size(axis))
    route = [(i - distance, i) for i in devices if i - distance in devices]
    return lax.ppermute(block, axis, route)


def conv_silu(padded, weight, length):
    summed = jnp.zeros((length,) + padded.shape[1:], jnp.float32)
    for offset in range(weight.shape[0]):
        summed = summed + weight[offset] * padded[offset : offset + length].astype(jnp.float32)
    return jax.nn.silu(summed).astype(jnp.bfloat16)


def local(
    x_input,
    z_input,
    bc_input,
    conv_weight_x,
    conv_weight_bc,
    step_size,
    log_decay,
    skip_gain,
    norm_gain,
    out_weight,
):
    length = x_input.shape[0]
    width = x_input.shape[1]
    groups = bc_input.shape[1]
    per_group = step_size.shape[1] // groups
    lead_rows = KCONV - 1
    highest = lax.Precision.HIGHEST
    prior_x, prior_bc = from_behind(
        (x_input[length - lead_rows :], bc_input[length - lead_rows :]), "seq", 1
    )
    x_conv = conv_silu(jnp.concatenate([prior_x, x_input], 0), conv_weight_x, length)
    bc_conv = conv_silu(jnp.concatenate([prior_bc, bc_input], 0), conv_weight_bc, length)
    blocks = length // BLOCK_LEN
    x_float = x_conv.astype(jnp.float32).reshape(blocks, BLOCK_LEN, groups, per_group, P_SIZE)
    bc_blocks = bc_conv.reshape(blocks, BLOCK_LEN, groups, 2 * N)
    b_half = bc_blocks[..., :N]
    c_half = bc_blocks[..., N:]
    b_mat = b_half.astype(jnp.float32)
    c_mat = c_half.astype(jnp.float32)
    driven = step_size.reshape(blocks, BLOCK_LEN, groups, per_group)[..., None] * x_float
    cumulative = jnp.cumsum(log_decay.reshape(blocks, BLOCK_LEN, groups, per_group), axis=1)
    lower_mask = jnp.tril(jnp.ones((BLOCK_LEN, BLOCK_LEN), bool))[None, :, :, None, None]
    log_gap = cumulative[:, :, None] - cumulative[:, None, :]
    decay_table = jnp.where(lower_mask, jnp.exp(jnp.where(lower_mask, log_gap, 0.0)), 0.0)
    scores = jnp.einsum("ctgn,csgn->ctsg", c_half, b_half, preferred_element_type=jnp.float32)
    within = jnp.einsum(
        "ctsgh,csghp->ctghp", scores[..., None] * decay_table, driven, precision=highest
    )
    last_log = cumulative[:, -1]
    fading = jnp.exp(last_log[:, None] - cumulative)[..., None] * driven
    block_states = jnp.einsum("csgn,csghp->cghnp", b_mat, fading, precision=highest)

    def pass_block(carry_state, pair):
        log_total, fresh = pair
        return (jnp.exp(log_total)[..., None, None] * carry_state + fresh, carry_state)

    empty_state = jnp.zeros((groups, per_group, N, P_SIZE), jnp.float32)
    final_state, entering = lax.scan(pass_block, empty_state, (last_log, block_states))
    offsets = jnp.cumsum(last_log, axis=0) - last_log
    device_log = jnp.sum(last_log, axis=0)

    def relay_turn(turn_index, incoming_state):
        return from_behind(
            jnp.exp(device_log)[..., None, None] * incoming_state + final_state, "seq", 1
        )

    incoming = lax.fori_loop(0, lax.axis_size("seq") - 1, relay_turn, empty_state)
    entering = entering + jnp.exp(offsets)[..., None, None] * incoming[None]
    carried = jnp.exp(cumulative)[..., None] * jnp.einsum(
        "ctgn,cghnp->ctghp", c_mat, entering, precision=highest
    )
    mixed = within + carried + skip_gain.reshape(groups, per_group)[..., None] * x_float
    gated_out = mixed.reshape(length, width) * jax.nn.silu(z_input.astype(jnp.float32))
    grouped = gated_out.reshape(length, groups, width // groups)
    normed = grouped * lax.rsqrt(jnp.mean(grouped * grouped, axis=-1, keepdims=True) + EPS)
    normed = (normed.reshape(length, width) * norm_gain).astype(jnp.bfloat16)
    result = lax.psum_scatter(
        jnp.dot(normed, out_weight, preferred_element_type=jnp.float32),
        "head",
        scatter_dimension=0,
        tiled=True,
    )
    return result.astype(jnp.bfloat16)


def solution(mesh):
    in_specs = (
        P("seq", "head"),
        P("seq", "head"),
        P("seq", "head", None),
        P(None, "head"),
        P(None, "head", None),
        P("seq", "head"),
        P("seq", "head"),
        P("head"),
        P("head"),
        P("head", None),
    )
    out_specs = P(("seq", "head"), None)
    return jax.shard_map(local, mesh=mesh, in_specs=in_specs, out_specs=out_specs, check_vma=False)
```

profile of v0, /device:TPU:1, one launch (start us, length us, event | category | flops | bytes accessed | tf_op | source)
XLA Modules:
  0.0 950.2 jit_solution(553629677135000963)
XLA Ops:
  51.5 17.2 %fusion.33 = f32[1024,2048]{0,1:T(8,128)} fusion(bf16[1024,2048]{0,1:T(8,128)(2,1)} %copy.62, f32[2048]{0:T(1024)S(1)} %bitcast.106, bf16[3,2048]{0,1:T(8,128)(2,1)} %collective-permute-done.1, f32[2048]{0:T(1024)S(1)} %bitcast.107, f32[2048]{0:T(1024)S(1)} %bitcast.105, f32[2048]{0:T(1024)S(1)} %bitcast.104), kind=kLoop, calls=%fused_computation.48 | loop fusion | flops 54525952 | bytes 12627968 | tf_op jit(solution)/shard_map/reshape | solution.py:52
  93.4 26.9 %while.26 = (s32[]{:T(128)}, f32[2,16,128,64]{3,2,1,0:T(8,128)S(1)}, f32[4,2,16,128,64]{4,3,2,1,0:T(8,128)}, f32[4,2,16]{2,1,0:T(2,128)S(1)}, f32[4,2,16,128,64]{3,4,2,1,0:T(8,128)}, /*index=5*/s32[]{:T(128)}, s32[]{:T(128)}) while((s32[]{:T(128)}, f32[2,16,128,64]{3,2,1,0:T(8,128)S(1)}, f32[4,2,16,128,64]{4,3,2,1,0:T(8,128)}, ...), condition=%wide.region_3.4_spmd.clone, body=%wide.region_2.3_spmd.clone.sunk | while | flops 1048579 | bytes 10486752 | solution.py:76
  121.1 516.0 %while.25 = (s32[]{:T(128)}, f32[2,16,128,64]{2,3,1,0:T(8,128)S(1)}, f32[2,16,1,1]{1,0,3,2:T(2,128)S(1)}, f32[2,16,128,64]{2,3,1,0:T(8,128)S(1)}, s32[]{:T(128)}) while((s32[]{:T(128)}, f32[2,16,128,64]{2,3,1,0:T(8,128)S(1)}, f32[2,16,1,1]{1,0,3,2:T(2,128)S(1)}, f32[2,16,128,64]{2,3,1,0:T(8,128)S(1)}, s32[]{:T(128)}) %tuple.60), condition=%wide.region_7.8_spmd, body=%wide.region_6.7_spmd.sunk | while | flops 524290 | bytes 7340261 | solution.py:85
  125.2 11.7 %collective-permute-done = f32[2,16,128,64]{2,3,1,0:T(8,128)S(1)} collective-permute-done((f32[2,16,128,64]{2,3,1,0:T(8,128)S(1)}, f32[2,16,128,64]{2,3,1,0:T(8,128)S(1)}, u32[]{:S(2)}, u32[]{:S(2)}) %collective-permute-start) | collective-permute-done | bytes 1048608 | tf_op jit(solution)/shard_map/while/body/eval_jaxpr/ppermute | solution.py:18
  141.5 11.7 %collective-permute-done = f32[2,16,128,64]{2,3,1,0:T(8,128)S(1)} collective-permute-done((f32[2,16,128,64]{2,3,1,0:T(8,128)S(1)}, f32[2,16,128,64]{2,3,1,0:T(8,128)S(1)}, u32[]{:S(2)}, u32[]{:S(2)}) %collective-permute-start) | collective-permute-done | bytes 1048608 | tf_op jit(solution)/shard_map/while/body/eval_jaxpr/ppermute | solution.py:18
  157.8 11.7 %collective-permute-done = f32[2,16,128,64]{2,3,1,0:T(8,128)S(1)} collective-permute-done((f32[2,16,128,64]{2,3,1,0:T(8,128)S(1)}, f32[2,16,128,64]{2,3,1,0:T(8,128)S(1)}, u32[]{:S(2)}, u32[]{:S(2)}) %collective-permute-start) | collective-permute-done | bytes 1048608 | tf_op jit(solution)/shard_map/while/body/eval_jaxpr/ppermute | solution.py:18
  174.1 11.7 %collective-permute-done = f32[2,16,128,64]{2,3,1,0:T(8,128)S(1)} collective-permute-done((f32[2,16,128,64]{2,3,1,0:T(8,128)S(1)}, f32[2,16,128,64]{2,3,1,0:T(8,128)S(1)}, u32[]{:S(2)}, u32[]{:S(2)}) %collective-permute-start) | collective-permute-done | bytes 1048608 | tf_op jit(solution)/shard_map/while/body/eval_jaxpr/ppermute | solution.py:18
  190.4 11.7 %collective-permute-done = f32[2,16,128,64]{2,3,1,0:T(8,128)S(1)} collective-permute-done((f32[2,16,128,64]{2,3,1,0:T(8,128)S(1)}, f32[2,16,128,64]{2,3,1,0:T(8,128)S(1)}, u32[]{:S(2)}, u32[]{:S(2)}) %collective-permute-start) | collective-permute-done | bytes 1048608 | tf_op jit(solution)/shard_map/while/body/eval_jaxpr/ppermute | solution.py:18
  206.6 11.7 %collective-permute-done = f32[2,16,128,64]{2,3,1,0:T(8,128)S(1)} collective-permute-done((f32[2,16,128,64]{2,3,1,0:T(8,128)S(1)}, f32[2,16,128,64]{2,3,1,0:T(8,128)S(1)}, u32[]{:S(2)}, u32[]{:S(2)}) %collective-permute-start) | collective-permute-done | bytes 1048608 | tf_op jit(solution)/shard_map/while/body/eval_jaxpr/ppermute | solution.py:18
  222.9 11.7 %collective-permute-done = f32[2,16,128,64]{2,3,1,0:T(8,128)S(1)} collective-permute-done((f32[2,16,128,64]{2,3,1,0:T(8,128)S(1)}, f32[2,16,128,64]{2,3,1,0:T(8,128)S(1)}, u32[]{:S(2)}, u32[]{:S(2)}) %collective-permute-start) | collective-permute-done | bytes 1048608 | tf_op jit(solution)/shard_map/while/body/eval_jaxpr/ppermute | solution.py:18
  255.5 11.7 %collective-permute-done = f32[2,16,128,64]{2,3,1,0:T(8,128)S(1)} collective-permute-done((f32[2,16,128,64]{2,3,1,0:T(8,128)S(1)}, f32[2,16,128,64]{2,3,1,0:T(8,128)S(1)}, u32[]{:S(2)}, u32[]{:S(2)}) %collective-permute-start) | collective-permute-done | bytes 1048608 | tf_op jit(solution)/shard_map/while/body/eval_jaxpr/ppermute | solution.py:18
  271.8 11.7 %collective-permute-done = f32[2,16,128,64]{2,3,1,0:T(8,128)S(1)} collective-permute-done((f32[2,16,128,64]{2,3,1,0:T(8,128)S(1)}, f32[2,16,128,64]{2,3,1,0:T(8,128)S(1)}, u32[]{:S(2)}, u32[]{:S(2)}) %collective-permute-start) | collective-permute-done | bytes 1048608 | tf_op jit(solution)/shard_map/while/body/eval_jaxpr/ppermute | solution.py:18
  304.4 11.7 %collective-permute-done = f32[2,16,128,64]{2,3,1,0:T(8,128)S(1)} collective-permute-done((f32[2,16,128,64]{2,3,1,0:T(8,128)S(1)}, f32[2,16,128,64]{2,3,1,0:T(8,128)S(1)}, u32[]{:S(2)}, u32[]{:S(2)}) %collective-permute-start) | collective-permute-done | bytes 1048608 | tf_op jit(solution)/shard_map/while/body/eval_jaxpr/ppermute | solution.py:18
  320.7 11.7 %collective-permute-done = f32[2,16,128,64]{2,3,1,0:T(8,128)S(1)} collective-permute-done((f32[2,16,128,64]{2,3,1,0:T(8,128)S(1)}, f32[2,16,128,64]{2,3,1,0:T(8,128)S(1)}, u32[]{:S(2)}, u32[]{:S(2)}) %collective-permute-start) | collective-permute-done | bytes 1048608 | tf_op jit(solution)/shard_map/while/body/eval_jaxpr/ppermute | solution.py:18
  353.3 11.7 %collective-permute-done = f32[2,16,128,64]{2,3,1,0:T(8,128)S(1)} collective-permute-done((f32[2,16,128,64]{2,3,1,0:T(8,128)S(1)}, f32[2,16,128,64]{2,3,1,0:T(8,128)S(1)}, u32[]{:S(2)}, u32[]{:S(2)}) %collective-permute-start) | collective-permute-done | bytes 1048608 | tf_op jit(solution)/shard_map/while/body/eval_jaxpr/ppermute | solution.py:18
  369.5 11.7 %collective-permute-done = f32[2,16,128,64]{2,3,1,0:T(8,128)S(1)} collective-permute-done((f32[2,16,128,64]{2,3,1,0:T(8,128)S(1)}, f32[2,16,128,64]{2,3,1,0:T(8,128)S(1)}, u32[]{:S(2)}, u32[]{:S(2)}) %collective-permute-start) | collective-permute-done | bytes 1048608 | tf_op jit(solution)/shard_map/while/body/eval_jaxpr/ppermute | solution.py:18
  385.8 11.7 %collective-permute-done = f32[2,16,128,64]{2,3,1,0:T(8,128)S(1)} collective-permute-done((f32[2,16,128,64]{2,3,1,0:T(8,128)S(1)}, f32[2,16,128,64]{2,3,1,0:T(8,128)S(1)}, u32[]{:S(2)}, u32[]{:S(2)}) %collective-permute-start) | collective-permute-done | bytes 1048608 | tf_op jit(solution)/shard_map/while/body/eval_jaxpr/ppermute | solution.py:18
  402.1 11.7 %collective-permute-done = f32[2,16,128,64]{2,3,1,0:T(8,128)S(1)} collective-permute-done((f32[2,16,128,64]{2,3,1,0:T(8,128)S(1)}, f32[2,16,128,64]{2,3,1,0:T(8,128)S(1)}, u32[]{:S(2)}, u32[]{:S(2)}) %collective-permute-start) | collective-permute-done | bytes 1048608 | tf_op jit(solution)/shard_map/while/body/eval_jaxpr/ppermute | solution.py:18
  418.4 11.7 %collective-permute-done = f32[2,16,128,64]{2,3,1,0:T(8,128)S(1)} collective-permute-done((f32[2,16,128,64]{2,3,1,0:T(8,128)S(1)}, f32[2,16,128,64]{2,3,1,0:T(8,128)S(1)}, u32[]{:S(2)}, u32[]{:S(2)}) %collective-permute-start) | collective-permute-done | bytes 1048608 | tf_op jit(solution)/shard_map/while/body/eval_jaxpr/ppermute | solution.py:18
  434.7 11.7 %collective-permute-done = f32[2,16,128,64]{2,3,1,0:T(8,128)S(1)} collective-permute-done((f32[2,16,128,64]{2,3,1,0:T(8,128)S(1)}, f32[2,16,128,64]{2,3,1,0:T(8,128)S(1)}, u32[]{:S(2)}, u32[]{:S(2)}) %collective-permute-start) | collective-permute-done | bytes 1048608 | tf_op jit(solution)/shard_map/while/body/eval_jaxpr/ppermute | solution.py:18
  467.3 11.7 %collective-permute-done = f32[2,16,128,64]{2,3,1,0:T(8,128)S(1)} collective-permute-done((f32[2,16,128,64]{2,3,1,0:T(8,128)S(1)}, f32[2,16,128,64]{2,3,1,0:T(8,128)S(1)}, u32[]{:S(2)}, u32[]{:S(2)}) %collective-permute-start) | collective-permute-done | bytes 1048608 | tf_op jit(solution)/shard_map/while/body/eval_jaxpr/ppermute | solution.py:18
  483.6 11.7 %collective-permute-done = f32[2,16,128,64]{2,3,1,0:T(8,128)S(1)} collective-permute-done((f32[2,16,128,64]{2,3,1,0:T(8,128)S(1)}, f32[2,16,128,64]{2,3,1,0:T(8,128)S(1)}, u32[]{:S(2)}, u32[]{:S(2)}) %collective-permute-start) | collective-permute-done | bytes 1048608 | tf_op jit(solution)/shard_map/while/body/eval_jaxpr/ppermute | solution.py:18
  516.1 11.7 %collective-permute-done = f32[2,16,128,64]{2,3,1,0:T(8,128)S(1)} collective-permute-done((f32[2,16,128,64]{2,3,1,0:T(8,128)S(1)}, f32[2,16,128,64]{2,3,1,0:T(8,128)S(1)}, u32[]{:S(2)}, u32[]{:S(2)}) %collective-permute-start) | collective-permute-done | bytes 1048608 | tf_op jit(solution)/shard_map/while/body/eval_jaxpr/ppermute | solution.py:18
  533.4 11.7 %collective-permute-done = f32[2,16,128,64]{2,3,1,0:T(8,128)S(1)} collective-permute-done((f32[2,16,128,64]{2,3,1,0:T(8,128)S(1)}, f32[2,16,128,64]{2,3,1,0:T(8,128)S(1)}, u32[]{:S(2)}, u32[]{:S(2)}) %collective-permute-start) | collective-permute-done | bytes 1048608 | tf_op jit(solution)/shard_map/while/body/eval_jaxpr/ppermute | solution.py:18
  551.8 11.7 %collective-permute-done = f32[2,16,128,64]{2,3,1,0:T(8,128)S(1)} collective-permute-done((f32[2,16,128,64]{2,3,1,0:T(8,128)S(1)}, f32[2,16,128,64]{2,3,1,0:T(8,128)S(1)}, u32[]{:S(2)}, u32[]{:S(2)}) %collective-permute-start) | collective-permute-done | bytes 1048608 | tf_op jit(solution)/shard_map/while/body/eval_jaxpr/ppermute | solution.py:18
  570.2 11.7 %collective-permute-done = f32[2,16,128,64]{2,3,1,0:T(8,128)S(1)} collective-permute-done((f32[2,16,128,64]{2,3,1,0:T(8,128)S(1)}, f32[2,16,128,64]{2,3,1,0:T(8,128)S(1)}, u32[]{:S(2)}, u32[]{:S(2)}) %collective-permute-start) | collective-permute-done | bytes 1048608 | tf_op jit(solution)/shard_map/while/body/eval_jaxpr/ppermute | solution.py:18
  588.6 11.7 %collective-permute-done = f32[2,16,128,64]{2,3,1,0:T(8,128)S(1)} collective-permute-done((f32[2,16,128,64]{2,3,1,0:T(8,128)S(1)}, f32[2,16,128,64]{2,3,1,0:T(8,128)S(1)}, u32[]{:S(2)}, u32[]{:S(2)}) %collective-permute-start) | collective-permute-done | bytes 1048608 | tf_op jit(solution)/shard_map/while/body/eval_jaxpr/ppermute | solution.py:18
  625.4 11.7 %collective-permute-done = f32[2,16,128,64]{2,3,1,0:T(8,128)S(1)} collective-permute-done((f32[2,16,128,64]{2,3,1,0:T(8,128)S(1)}, f32[2,16,128,64]{2,3,1,0:T(8,128)S(1)}, u32[]{:S(2)}, u32[]{:S(2)}) %collective-permute-start) | collective-permute-done | bytes 1048608 | tf_op jit(solution)/shard_map/while/body/eval_jaxpr/ppermute | solution.py:18
  647.9 42.0 %fusion.18 = f32[4,256,2,16,64]{1,4,3,2,0:T(8,128)} fusion(f32[4,2,16,64,256]{4,3,2,1,0:T(8,128)S(1)} %fusion.22, f32[4,256,2,16,64]{1,0,4,3,2:T(4,128)} %reshape.90, f32[4,256,2,16]{1,3,2,0:T(8,128)S(1)} %bitcast_bitcast_fusion, f32[4,256,256,2]{2,1,3,0:T(8,128)S(1)} %copy-done.2, pred[256,256]{1,0:T(8,128)(4,1)S(1)} %copy-done.4, ...), kind=kOutput, calls=%fused_computation.28 | convolution fusion | flops 6484393984 | bytes 35979392 | tf_op jit(solution)/shard_map/ctsgh,csghp->ctghp/dot_general | solution.py:64
  689.9 13.8 %copy.83 = f32[4,256,2,16,64]{1,0,4,3,2:T(4,128)} copy(f32[4,256,2,16,64]{1,4,3,2,0:T(8,128)} %fusion.18) | data formatting | bytes 16777216 | tf_op jit(solution)/shard_map/add | solution.py:90
  715.2 22.9 %fusion.52 = f32[1024,4096]{1,0:T(8,128)} fusion(bf16[1024,2048]{0,1:T(8,128)(2,1)S(1)} %fusion.16, bf16[2048,4096]{1,0:T(8,128)(2,1)} %param.23), kind=kOutput, calls=%fused_computation.85 | convolution fusion | flops 17179869184 | bytes 37748736 | tf_op jit(solution)/shard_map/dot_general | solution.py:96
  738.2 201.2 %reduce-scatter.2.cloned.1.call-done = f32[256,4096]{1,0:T(8,128)} async-done(((f32[1024,4096]{1,0:T(8,128)}), f32[256,4096]{1,0:T(8,128)}) %reduce-scatter.2.cloned.1.call-update) | async-done | bytes 4194320 | tf_op jit(solution)/shard_map/reduce_scatter | solution.py:95
  (159 shorter events, 345.5 us)
Async XLA Ops:
  6.5 932.8 %reduce-scatter.2.cloned.1.call-start = ((), (), s32[]{:S(2)}) async-start(), calls=%async_computation.1 | async-start | bytes 20971520 | tf_op jit(solution)/shard_map/reduce_scatter | solution.py:95
  8.4 43.1 %collective-permute-start.1 = (bf16[3,2048]{0,1:T(8,128)(2,1)}, bf16[3,2048]{0,1:T(8,128)(2,1)}, u32[]{:S(2)}, u32[]{:S(2)}) collective-permute-start(bf16[3,2048]{0,1:T(8,128)(2,1)} %copy.61), channel_id=1, source_target_pairs={{0,4},{4,8},{8,12},{12,16},{16,20},{20,24},{24,28},{28,32},{32,36}... | collective-permute-start | bytes 36872 | tf_op jit(solution)/shard_map/ppermute | solution.py:18
  15.3 28.1 %collective-permute-start.2 = (bf16[3,2,256]{2,0,1:T(4,128)(2,1)}, bf16[3,2,256]{2,0,1:T(4,128)(2,1)}, u32[]{:S(2)}, u32[]{:S(2)}) collective-permute-start(bf16[3,2,256]{2,0,1:T(4,128)(2,1)} %slice.88), channel_id=1, source_target_pairs={{0,4},{4,8},{8,12},{12,16},{16,20},{20,24},{24,28},{28,32},{32,36}... | collective-permute-start | bytes 9224 | tf_op jit(solution)/shard_map/ppermute | solution.py:18
  137.1 16.1 %collective-permute-start = (f32[2,16,128,64]{2,3,1,0:T(8,128)S(1)}, f32[2,16,128,64]{2,3,1,0:T(8,128)S(1)}, u32[]{:S(2)}, u32[]{:S(2)}) collective-permute-start(f32[2,16,128,64]{2,3,1,0:T(8,128)S(1)} %multiply_add_fusion.2), channel_id=1, source_target_pairs={{0,4},{4,8},{8,12},{12,16},{16,20},{20,24},{24,28},{28,32},{32,36}... | collective-permute-start | bytes 3145736 | tf_op jit(solution)/shard_map/while/body/eval_jaxpr/ppermute | solution.py:18
  153.4 16.1 %collective-permute-start = (f32[2,16,128,64]{2,3,1,0:T(8,128)S(1)}, f32[2,16,128,64]{2,3,1,0:T(8,128)S(1)}, u32[]{:S(2)}, u32[]{:S(2)}) collective-permute-start(f32[2,16,128,64]{2,3,1,0:T(8,128)S(1)} %multiply_add_fusion.2), channel_id=1, source_target_pairs={{0,4},{4,8},{8,12},{12,16},{16,20},{20,24},{24,28},{28,32},{32,36}... | collective-permute-start | bytes 3145736 | tf_op jit(solution)/shard_map/while/body/eval_jaxpr/ppermute | solution.py:18
  169.7 16.1 %collective-permute-start = (f32[2,16,128,64]{2,3,1,0:T(8,128)S(1)}, f32[2,16,128,64]{2,3,1,0:T(8,128)S(1)}, u32[]{:S(2)}, u32[]{:S(2)}) collective-permute-start(f32[2,16,128,64]{2,3,1,0:T(8,128)S(1)} %multiply_add_fusion.2), channel_id=1, source_target_pairs={{0,4},{4,8},{8,12},{12,16},{16,20},{20,24},{24,28},{28,32},{32,36}... | collective-permute-start | bytes 3145736 | tf_op jit(solution)/shard_map/while/body/eval_jaxpr/ppermute | solution.py:18
  186.0 16.1 %collective-permute-start = (f32[2,16,128,64]{2,3,1,0:T(8,128)S(1)}, f32[2,16,128,64]{2,3,1,0:T(8,128)S(1)}, u32[]{:S(2)}, u32[]{:S(2)}) collective-permute-start(f32[2,16,128,64]{2,3,1,0:T(8,128)S(1)} %multiply_add_fusion.2), channel_id=1, source_target_pairs={{0,4},{4,8},{8,12},{12,16},{16,20},{20,24},{24,28},{28,32},{32,36}... | collective-permute-start | bytes 3145736 | tf_op jit(solution)/shard_map/while/body/eval_jaxpr/ppermute | solution.py:18
  202.2 16.1 %collective-permute-start = (f32[2,16,128,64]{2,3,1,0:T(8,128)S(1)}, f32[2,16,128,64]{2,3,1,0:T(8,128)S(1)}, u32[]{:S(2)}, u32[]{:S(2)}) collective-permute-start(f32[2,16,128,64]{2,3,1,0:T(8,128)S(1)} %multiply_add_fusion.2), channel_id=1, source_target_pairs={{0,4},{4,8},{8,12},{12,16},{16,20},{20,24},{24,28},{28,32},{32,36}... | collective-permute-start | bytes 3145736 | tf_op jit(solution)/shard_map/while/body/eval_jaxpr/ppermute | solution.py:18
  218.5 16.1 %collective-permute-start = (f32[2,16,128,64]{2,3,1,0:T(8,128)S(1)}, f32[2,16,128,64]{2,3,1,0:T(8,128)S(1)}, u32[]{:S(2)}, u32[]{:S(2)}) collective-permute-start(f32[2,16,128,64]{2,3,1,0:T(8,128)S(1)} %multiply_add_fusion.2), channel_id=1, source_target_pairs={{0,4},{4,8},{8,12},{12,16},{16,20},{20,24},{24,28},{28,32},{32,36}... | collective-permute-start | bytes 3145736 | tf_op jit(solution)/shard_map/while/body/eval_jaxpr/ppermute | solution.py:18
  234.8 16.1 %collective-permute-start = (f32[2,16,128,64]{2,3,1,0:T(8,128)S(1)}, f32[2,16,128,64]{2,3,1,0:T(8,128)S(1)}, u32[]{:S(2)}, u32[]{:S(2)}) collective-permute-start(f32[2,16,128,64]{2,3,1,0:T(8,128)S(1)} %multiply_add_fusion.2), channel_id=1, source_target_pairs={{0,4},{4,8},{8,12},{12,16},{16,20},{20,24},{24,28},{28,32},{32,36}... | collective-permute-start | bytes 3145736 | tf_op jit(solution)/shard_map/while/body/eval_jaxpr/ppermute | solution.py:18
  251.1 16.1 %collective-permute-start = (f32[2,16,128,64]{2,3,1,0:T(8,128)S(1)}, f32[2,16,128,64]{2,3,1,0:T(8,128)S(1)}, u32[]{:S(2)}, u32[]{:S(2)}) collective-permute-start(f32[2,16,128,64]{2,3,1,0:T(8,128)S(1)} %multiply_add_fusion.2), channel_id=1, source_target_pairs={{0,4},{4,8},{8,12},{12,16},{16,20},{20,24},{24,28},{28,32},{32,36}... | collective-permute-start | bytes 3145736 | tf_op jit(solution)/shard_map/while/body/eval_jaxpr/ppermute | solution.py:18
  267.4 16.1 %collective-permute-start = (f32[2,16,128,64]{2,3,1,0:T(8,128)S(1)}, f32[2,16,128,64]{2,3,1,0:T(8,128)S(1)}, u32[]{:S(2)}, u32[]{:S(2)}) collective-permute-start(f32[2,16,128,64]{2,3,1,0:T(8,128)S(1)} %multiply_add_fusion.2), channel_id=1, source_target_pairs={{0,4},{4,8},{8,12},{12,16},{16,20},{20,24},{24,28},{28,32},{32,36}... | collective-permute-start | bytes 3145736 | tf_op jit(solution)/shard_map/while/body/eval_jaxpr/ppermute | solution.py:18
  283.7 16.1 %collective-permute-start = (f32[2,16,128,64]{2,3,1,0:T(8,128)S(1)}, f32[2,16,128,64]{2,3,1,0:T(8,128)S(1)}, u32[]{:S(2)}, u32[]{:S(2)}) collective-permute-start(f32[2,16,128,64]{2,3,1,0:T(8,128)S(1)} %multiply_add_fusion.2), channel_id=1, source_target_pairs={{0,4},{4,8},{8,12},{12,16},{16,20},{20,24},{24,28},{28,32},{32,36}... | collective-permute-start | bytes 3145736 | tf_op jit(solution)/shard_map/while/body/eval_jaxpr/ppermute | solution.py:18
  300.0 16.1 %collective-permute-start = (f32[2,16,128,64]{2,3,1,0:T(8,128)S(1)}, f32[2,16,128,64]{2,3,1,0:T(8,128)S(1)}, u32[]{:S(2)}, u32[]{:S(2)}) collective-permute-start(f32[2,16,128,64]{2,3,1,0:T(8,128)S(1)} %multiply_add_fusion.2), channel_id=1, source_target_pairs={{0,4},{4,8},{8,12},{12,16},{16,20},{20,24},{24,28},{28,32},{32,36}... | collective-permute-start | bytes 3145736 | tf_op jit(solution)/shard_map/while/body/eval_jaxpr/ppermute | solution.py:18
  316.3 16.1 %collective-permute-start = (f32[2,16,128,64]{2,3,1,0:T(8,128)S(1)}, f32[2,16,128,64]{2,3,1,0:T(8,128)S(1)}, u32[]{:S(2)}, u32[]{:S(2)}) collective-permute-start(f32[2,16,128,64]{2,3,1,0:T(8,128)S(1)} %multiply_add_fusion.2), channel_id=1, source_target_pairs={{0,4},{4,8},{8,12},{12,16},{16,20},{20,24},{24,28},{28,32},{32,36}... | collective-permute-start | bytes 3145736 | tf_op jit(solution)/shard_map/while/body/eval_jaxpr/ppermute | solution.py:18
  332.6 16.1 %collective-permute-start = (f32[2,16,128,64]{2,3,1,0:T(8,128)S(1)}, f32[2,16,128,64]{2,3,1,0:T(8,128)S(1)}, u32[]{:S(2)}, u32[]{:S(2)}) collective-permute-start(f32[2,16,128,64]{2,3,1,0:T(8,128)S(1)} %multiply_add_fusion.2), channel_id=1, source_target_pairs={{0,4},{4,8},{8,12},{12,16},{16,20},{20,24},{24,28},{28,32},{32,36}... | collective-permute-start | bytes 3145736 | tf_op jit(solution)/shard_map/while/body/eval_jaxpr/ppermute | solution.py:18
  348.9 16.1 %collective-permute-start = (f32[2,16,128,64]{2,3,1,0:T(8,128)S(1)}, f32[2,16,128,64]{2,3,1,0:T(8,128)S(1)}, u32[]{:S(2)}, u32[]{:S(2)}) collective-permute-start(f32[2,16,128,64]{2,3,1,0:T(8,128)S(1)} %multiply_add_fusion.2), channel_id=1, source_target_pairs={{0,4},{4,8},{8,12},{12,16},{16,20},{20,24},{24,28},{28,32},{32,36}... | collective-permute-start | bytes 3145736 | tf_op jit(solution)/shard_map/while/body/eval_jaxpr/ppermute | solution.py:18
  365.1 16.1 %collective-permute-start = (f32[2,16,128,64]{2,3,1,0:T(8,128)S(1)}, f32[2,16,128,64]{2,3,1,0:T(8,128)S(1)}, u32[]{:S(2)}, u32[]{:S(2)}) collective-permute-start(f32[2,16,128,64]{2,3,1,0:T(8,128)S(1)} %multiply_add_fusion.2), channel_id=1, source_target_pairs={{0,4},{4,8},{8,12},{12,16},{16,20},{20,24},{24,28},{28,32},{32,36}... | collective-permute-start | bytes 3145736 | tf_op jit(solution)/shard_map/while/body/eval_jaxpr/ppermute | solution.py:18
  381.4 16.1 %collective-permute-start = (f32[2,16,128,64]{2,3,1,0:T(8,128)S(1)}, f32[2,16,128,64]{2,3,1,0:T(8,128)S(1)}, u32[]{:S(2)}, u32[]{:S(2)}) collective-permute-start(f32[2,16,128,64]{2,3,1,0:T(8,128)S(1)} %multiply_add_fusion.2), channel_id=1, source_target_pairs={{0,4},{4,8},{8,12},{12,16},{16,20},{20,24},{24,28},{28,32},{32,36}... | collective-permute-start | bytes 3145736 | tf_op jit(solution)/shard_map/while/body/eval_jaxpr/ppermute | solution.py:18
  397.7 16.1 %collective-permute-start = (f32[2,16,128,64]{2,3,1,0:T(8,128)S(1)}, f32[2,16,128,64]{2,3,1,0:T(8,128)S(1)}, u32[]{:S(2)}, u32[]{:S(2)}) collective-permute-start(f32[2,16,128,64]{2,3,1,0:T(8,128)S(1)} %multiply_add_fusion.2), channel_id=1, source_target_pairs={{0,4},{4,8},{8,12},{12,16},{16,20},{20,24},{24,28},{28,32},{32,36}... | collective-permute-start | bytes 3145736 | tf_op jit(solution)/shard_map/while/body/eval_jaxpr/ppermute | solution.py:18
  414.0 16.1 %collective-permute-start = (f32[2,16,128,64]{2,3,1,0:T(8,128)S(1)}, f32[2,16,128,64]{2,3,1,0:T(8,128)S(1)}, u32[]{:S(2)}, u32[]{:S(2)}) collective-permute-start(f32[2,16,128,64]{2,3,1,0:T(8,128)S(1)} %multiply_add_fusion.2), channel_id=1, source_target_pairs={{0,4},{4,8},{8,12},{12,16},{16,20},{20,24},{24,28},{28,32},{32,36}... | collective-permute-start | bytes 3145736 | tf_op jit(solution)/shard_map/while/body/eval_jaxpr/ppermute | solution.py:18
  430.3 16.1 %collective-permute-start = (f32[2,16,128,64]{2,3,1,0:T(8,128)S(1)}, f32[2,16,128,64]{2,3,1,0:T(8,128)S(1)}, u32[]{:S(2)}, u32[]{:S(2)}) collective-permute-start(f32[2,16,128,64]{2,3,1,0:T(8,128)S(1)} %multiply_add_fusion.2), channel_id=1, source_target_pairs={{0,4},{4,8},{8,12},{12,16},{16,20},{20,24},{24,28},{28,32},{32,36}... | collective-permute-start | bytes 3145736 | tf_op jit(solution)/shard_map/while/body/eval_jaxpr/ppermute | solution.py:18
  446.6 16.1 %collective-permute-start = (f32[2,16,128,64]{2,3,1,0:T(8,128)S(1)}, f32[2,16,128,64]{2,3,1,0:T(8,128)S(1)}, u32[]{:S(2)}, u32[]{:S(2)}) collective-permute-start(f32[2,16,128,64]{2,3,1,0:T(8,128)S(1)} %multiply_add_fusion.2), channel_id=1, source_target_pairs={{0,4},{4,8},{8,12},{12,16},{16,20},{20,24},{24,28},{28,32},{32,36}... | collective-permute-start | bytes 3145736 | tf_op jit(solution)/shard_map/while/body/eval_jaxpr/ppermute | solution.py:18
  462.9 16.1 %collective-permute-start = (f32[2,16,128,64]{2,3,1,0:T(8,128)S(1)}, f32[2,16,128,64]{2,3,1,0:T(8,128)S(1)}, u32[]{:S(2)}, u32[]{:S(2)}) collective-permute-start(f32[2,16,128,64]{2,3,1,0:T(8,128)S(1)} %multiply_add_fusion.2), channel_id=1, source_target_pairs={{0,4},{4,8},{8,12},{12,16},{16,20},{20,24},{24,28},{28,32},{32,36}... | collective-permute-start | bytes 3145736 | tf_op jit(solution)/shard_map/while/body/eval_jaxpr/ppermute | solution.py:18
  479.2 16.1 %collective-permute-start = (f32[2,16,128,64]{2,3,1,0:T(8,128)S(1)}, f32[2,16,128,64]{2,3,1,0:T(8,128)S(1)}, u32[]{:S(2)}, u32[]{:S(2)}) collective-permute-start(f32[2,16,128,64]{2,3,1,0:T(8,128)S(1)} %multiply_add_fusion.2), channel_id=1, source_target_pairs={{0,4},{4,8},{8,12},{12,16},{16,20},{20,24},{24,28},{28,32},{32,36}... | collective-permute-start | bytes 3145736 | tf_op jit(solution)/shard_map/while/body/eval_jaxpr/ppermute | solution.py:18
  495.5 16.1 %collective-permute-start = (f32[2,16,128,64]{2,3,1,0:T(8,128)S(1)}, f32[2,16,128,64]{2,3,1,0:T(8,128)S(1)}, u32[]{:S(2)}, u32[]{:S(2)}) collective-permute-start(f32[2,16,128,64]{2,3,1,0:T(8,128)S(1)} %multiply_add_fusion.2), channel_id=1, source_target_pairs={{0,4},{4,8},{8,12},{12,16},{16,20},{20,24},{24,28},{28,32},{32,36}... | collective-permute-start | bytes 3145736 | tf_op jit(solution)/shard_map/while/body/eval_jaxpr/ppermute | solution.py:18
  528.0 17.0 %collective-permute-start = (f32[2,16,128,64]{2,3,1,0:T(8,128)S(1)}, f32[2,16,128,64]{2,3,1,0:T(8,128)S(1)}, u32[]{:S(2)}, u32[]{:S(2)}) collective-permute-start(f32[2,16,128,64]{2,3,1,0:T(8,128)S(1)} %multiply_add_fusion.2), channel_id=1, source_target_pairs={{0,4},{4,8},{8,12},{12,16},{16,20},{20,24},{24,28},{28,32},{32,36}... | collective-permute-start | bytes 3145736 | tf_op jit(solution)/shard_map/while/body/eval_jaxpr/ppermute | solution.py:18
  545.3 18.2 %collective-permute-start = (f32[2,16,128,64]{2,3,1,0:T(8,128)S(1)}, f32[2,16,128,64]{2,3,1,0:T(8,128)S(1)}, u32[]{:S(2)}, u32[]{:S(2)}) collective-permute-start(f32[2,16,128,64]{2,3,1,0:T(8,128)S(1)} %multiply_add_fusion.2), channel_id=1, source_target_pairs={{0,4},{4,8},{8,12},{12,16},{16,20},{20,24},{24,28},{28,32},{32,36}... | collective-permute-start | bytes 3145736 | tf_op jit(solution)/shard_map/while/body/eval_jaxpr/ppermute | solution.py:18
  563.7 18.2 %collective-permute-start = (f32[2,16,128,64]{2,3,1,0:T(8,128)S(1)}, f32[2,16,128,64]{2,3,1,0:T(8,128)S(1)}, u32[]{:S(2)}, u32[]{:S(2)}) collective-permute-start(f32[2,16,128,64]{2,3,1,0:T(8,128)S(1)} %multiply_add_fusion.2), channel_id=1, source_target_pairs={{0,4},{4,8},{8,12},{12,16},{16,20},{20,24},{24,28},{28,32},{32,36}... | collective-permute-start | bytes 3145736 | tf_op jit(solution)/shard_map/while/body/eval_jaxpr/ppermute | solution.py:18
  582.1 18.2 %collective-permute-start = (f32[2,16,128,64]{2,3,1,0:T(8,128)S(1)}, f32[2,16,128,64]{2,3,1,0:T(8,128)S(1)}, u32[]{:S(2)}, u32[]{:S(2)}) collective-permute-start(f32[2,16,128,64]{2,3,1,0:T(8,128)S(1)} %multiply_add_fusion.2), channel_id=1, source_target_pairs={{0,4},{4,8},{8,12},{12,16},{16,20},{20,24},{24,28},{28,32},{32,36}... | collective-permute-start | bytes 3145736 | tf_op jit(solution)/shard_map/while/body/eval_jaxpr/ppermute | solution.py:18
  600.4 18.2 %collective-permute-start = (f32[2,16,128,64]{2,3,1,0:T(8,128)S(1)}, f32[2,16,128,64]{2,3,1,0:T(8,128)S(1)}, u32[]{:S(2)}, u32[]{:S(2)}) collective-permute-start(f32[2,16,128,64]{2,3,1,0:T(8,128)S(1)} %multiply_add_fusion.2), channel_id=1, source_target_pairs={{0,4},{4,8},{8,12},{12,16},{16,20},{20,24},{24,28},{28,32},{32,36}... | collective-permute-start | bytes 3145736 | tf_op jit(solution)/shard_map/while/body/eval_jaxpr/ppermute | solution.py:18
  618.8 18.2 %collective-permute-start = (f32[2,16,128,64]{2,3,1,0:T(8,128)S(1)}, f32[2,16,128,64]{2,3,1,0:T(8,128)S(1)}, u32[]{:S(2)}, u32[]{:S(2)}) collective-permute-start(f32[2,16,128,64]{2,3,1,0:T(8,128)S(1)} %multiply_add_fusion.2), channel_id=1, source_target_pairs={{0,4},{4,8},{8,12},{12,16},{16,20},{20,24},{24,28},{28,32},{32,36}... | collective-permute-start | bytes 3145736 | tf_op jit(solution)/shard_map/while/body/eval_jaxpr/ppermute | solution.py:18
  (13 other events, 615.8 us)
Sparse Core Ops, SparseCore 0:
  738.3 201.0 reduce-scatter.1
where the time goes:
time: 961 us; the launch traced here: 950 us
  waiting for transfers between devices  564 us (59%)
  starting transfers between devices  154 us (16%)
  matrix products  82.6 us (9%)
  local copies, waits for them, and re-layouts  71.3 us (7%)
  other arithmetic  63.4 us (7%)
  between operations  13.9 us (1%)
    ppermute x33, waiting for transfers between devices, from_behind(): return lax.ppermute(block, axis, route)  363 us
    reduce_scatter x1, waiting for transfers between devices, local(): lax.psum_scatter(jnp.dot(normed, out_weight, preferred_element_type=jnp.f...  201 us
    ppermute x33, starting transfers between devices, from_behind(): return lax.ppermute(block, axis, route)  154 us
    dot_general x1, matrix products, local(): jnp.einsum('ctsgh,csghp->ctghp', scores[..., None] * decay_table, driven,...  42 us
    dot_general x1, matrix products, local(): jnp.dot(normed, out_weight, preferred_element_type=jnp.float32)  22.9 us
    unnamed x26, local copies, waits for them, and re-layouts  20.7 us
  transfers between devices with their start and end apart: 34, of which 32 were waited for; matrix products, arithmetic and copies ran while one was open for 4% of the time, Pallas kernels for 0%

commit v1 on v0

v1 whole, which is shorter than its diff:
```python
import functools

import jax
import jax.numpy as jnp
from jax import lax
from jax.experimental import pallas as pl
from jax.experimental.pallas import tpu as pltpu
from jax.sharding import PartitionSpec as P

P_SIZE = 64
N = 128
KCONV = 4
EPS = 1e-05
Q = 128
LEAD = 16
TILE = 256
PIECES = 4
HEADS = 4

MESH = pl.DeviceIdType.MESH
F32 = jnp.float32
BF16 = jnp.bfloat16


def split3(value):
    hi = value.astype(BF16)
    rest = value - hi.astype(F32)
    mid = rest.astype(BF16)
    return hi, mid, (rest - mid.astype(F32)).astype(BF16)


def dot(a, b):
    return jnp.dot(a, b, preferred_element_type=F32)


def silu(v):
    return v * (0.5 * jnp.tanh(0.5 * v) + 0.5)


def kernel(
    ns,
    x_hbm,
    z_hbm,
    bc_hbm,
    w_hbm,
    cwx,
    cwbc,
    step_ref,
    ld_ref,
    skip_ref,
    gain_ref,
    out_hbm,
    xb,
    zb,
    bcb,
    wb,
    ub,
    pst,
    fac,
    e4,
    a4,
    u4,
    em,
    et,
    eo,
    rt,
    skx,
    dl_all,
    dexp,
    fmsg,
    frecv,
    imsg,
    irecv,
    gbuf,
    rs_send,
    rs_recv,
    local_sem,
    halo_send,
    halo_recv,
    dl_s,
    dl_r,
    f_s,
    f_r,
    i_s,
    i_r,
    r_s,
    r_r,
    out_sem,
):
    length, width = x_hbm.shape
    columns = w_hbm.shape[1]
    heads = step_ref.shape[1]
    groups = bc_hbm.shape[1] // (2 * N)
    gw = width // groups
    blocks = length // Q
    chunk_rows = length // HEADS
    half = columns // 2
    piece = half // PIECES
    row_parts = N // 16
    col_parts = ns // row_parts
    part = width // col_parts

    me = lax.axis_index("seq")
    d = lax.axis_index("head")
    right = lax.rem(d + 1, HEADS)
    left = lax.rem(d + HEADS - 1, HEADS)
    after = lax.rem(me + 1, ns)

    barrier = pltpu.get_barrier_semaphore()

    def greet(k, carry):
        pl.semaphore_signal(barrier, inc=1, device_id=(lax.rem(me + k, ns), d), device_id_type=MESH)
        return carry

    lax.fori_loop(1, ns, greet, 0)
    for other in (right, left):
        pl.semaphore_signal(barrier, inc=1, device_id=(me, other), device_id_type=MESH)

    def load_x(g):
        return pltpu.make_async_copy(
            x_hbm.at[:, pl.ds(g * gw, gw)],
            xb.at[pl.ds(LEAD, length), pl.ds(g * gw, gw)],
            local_sem.at[g],
        )

    load_bc = pltpu.make_async_copy(bc_hbm, bcb.at[pl.ds(LEAD, length)], local_sem.at[2])
    load_z = pltpu.make_async_copy(z_hbm, zb, local_sem.at[3])

    def load_w(h):
        return pltpu.make_async_copy(
            w_hbm.at[:, pl.ds(h * half, half)], wb.at[:, pl.ds(h * half, half)], local_sem.at[4 + h]
        )

    load_bc.start()
    load_x(0).start()
    load_x(1).start()

    lanes = 128
    lane_row = lax.broadcasted_iota(jnp.int32, (lanes, TILE), 0)
    lane_col = lax.broadcasted_iota(jnp.int32, (lanes, TILE), 1)
    for tile in range(width // TILE):
        head = lax.div(lane_col + tile * TILE, P_SIZE)
        spread = (head == lax.rem(lane_row, heads)) & (lane_row < 3 * heads)
        e4[:, tile * TILE : (tile + 1) * TILE] = jnp.where(spread, 1.0, 0.0).astype(BF16)

    def pack(value):
        hi, mid, lo = split3(value)
        lane = lax.broadcasted_iota(jnp.int32, value.shape, 1)
        hi, mid, lo = hi.astype(F32), mid.astype(F32), lo.astype(F32)
        chosen = jnp.where(lane < heads, hi, jnp.where(lane < 2 * heads, mid, lo))
        return jnp.where(lane < 3 * heads, chosen, 0.0).astype(BF16)

    rep = jnp.where(
        lax.rem(lax.broadcasted_iota(jnp.int32, (heads, lanes), 1), heads)
        == lax.broadcasted_iota(jnp.int32, (heads, lanes), 0),
        1.0,
        0.0,
    ).astype(BF16)
    low = jnp.where(
        lax.broadcasted_iota(jnp.int32, (Q, Q), 0) >= lax.broadcasted_iota(jnp.int32, (Q, Q), 1), 1.0, 0.0
    ).astype(BF16)

    def exact(left_mat, parts):
        return dot(left_mat, parts[0]) + dot(left_mat, parts[1]) + dot(left_mat, parts[2])

    mids, tots = [], []
    for b in range(blocks):
        rows = slice(b * Q, (b + 1) * Q)
        parts = split3(ld_ref[rows, :])
        ld4 = dot(parts[0], rep) + dot(parts[1], rep) + dot(parts[2], rep)
        parts = split3(step_ref[rows, :])
        step4 = dot(parts[0], rep) + dot(parts[1], rep) + dot(parts[2], rep)
        cum = exact(low, split3(ld4))
        mid = cum[Q // 2 - 1 : Q // 2, :]
        a4[rows, :] = pack(jnp.exp(cum - mid))
        u4[rows, :] = pack(step4 * jnp.exp(mid - cum))
        mids.append(mid)
        tots.append(cum[Q - 1 : Q, :])
    row = lax.broadcasted_iota(jnp.int32, (blocks, lanes), 0)
    zero = jnp.zeros((blocks, lanes), F32)
    m8, t8, o8, s8 = zero, zero, zero, zero
    run = jnp.zeros((1, lanes), F32)
    for b in range(blocks):
        m8 = jnp.where(row == b, mids[b], m8)
        t8 = jnp.where(row == b, tots[b], t8)
        o8 = jnp.where(row == b, run, o8)
        run = run + tots[b]
    dl_all[me] = jnp.broadcast_to(run, (8, lanes))
    later = jnp.zeros((1, lanes), F32)
    for b in reversed(range(blocks)):
        s8 = jnp.where(row == b, later, s8)
        later = later + tots[b]

    pl.semaphore_wait(barrier, ns + 1)

    def halo(kind, src, dst):
        return pltpu.make_async_remote_copy(
            src_ref=src.at[pl.ds(length - LEAD, LEAD)],
            dst_ref=dst.at[pl.ds(0, LEAD)],
            send_sem=halo_send.at[kind],
            recv_sem=halo_recv.at[kind],
            device_id=(after, d),
            device_id_type=MESH,
        )

    halo(0, x_hbm, xb).start()
    halo(1, bc_hbm, bcb).start()

    def to_seq(src, dst, send, recv, slot, there, other):
        return pltpu.make_async_remote_copy(
            src_ref=src.at[slot],
            dst_ref=dst.at[there],
            send_sem=send.at[slot],
            recv_sem=recv.at[there],
            device_id=(other, d),
            device_id_type=MESH,
        )

    def decay_copy(j):
        return pltpu.make_async_remote_copy(
            src_ref=dl_all.at[me],
            dst_ref=dl_all.at[me],
            send_sem=dl_s.at[j],
            recv_sem=dl_r.at[me],
            device_id=(j, d),
            device_id_type=MESH,
        )

    def send_decay(k, carry):
        decay_copy(lax.rem(me + k, ns)).start()
        return carry

    lax.fori_loop(1, ns, send_decay, 0)

    for ref, value in (
        (em, jnp.exp(m8)),
        (et, jnp.exp(t8 - m8)),
        (eo, jnp.exp(o8)),
        (rt, jnp.exp(s8 + t8 - m8)),
    ):
        ref[...] = dot(pack(value), e4[...])
    parts = split3(jnp.broadcast_to(skip_ref[...], (8, heads)))
    skx[...] = dot(pack(dot(parts[0], rep) + dot(parts[1], rep) + dot(parts[2], rep)), e4[...])

    def conv(buf, weight, r0, cols):
        prev = buf[pl.ds(r0, LEAD), cols].astype(F32)[LEAD - 8 :]
        cur = buf[pl.ds(r0 + LEAD, Q), cols].astype(F32)
        ext = jnp.concatenate([prev, cur], 0)
        total = weight[KCONV - 1 : KCONV, cols] * cur
        for k in range(1, KCONV):
            total = total + weight[KCONV - 1 - k : KCONV - k, cols] * pltpu.roll(ext, k, 0)[8:]
        done = silu(total).astype(BF16)
        buf[pl.ds(r0 + LEAD, Q), cols] = done
        return done

    load_bc.wait()
    for g in range(groups):
        load_x(g).wait()
        if g == groups - 1:
            load_z.start()
            load_w(0).start()
            load_w(1).start()

        def first_pass(turn, carry, g=g):
            b = blocks - 1 - turn
            r0 = pl.multiple_of(b * Q, Q)

            if g == 0:

                @pl.when(b == 0)
                def _():
                    halo(0, x_hbm, xb).wait_recv()
                    halo(1, bc_hbm, bcb).wait_recv()

                    @pl.when(me == 0)
                    def _():
                        xb[:LEAD, :] = jnp.zeros((LEAD, width), BF16)
                        bcb[:LEAD, :] = jnp.zeros((LEAD, bcb.shape[1]), BF16)

            bc = conv(bcb, cwbc, r0, slice(g * 2 * N, (g + 1) * 2 * N))
            b_turned = bc[:, :N].astype(F32).T.astype(BF16)
            for tile in range(gw // TILE):
                cols = slice(g * gw + tile * TILE, g * gw + (tile + 1) * TILE)
                xc = conv(xb, cwx, r0, cols).astype(F32)
                u = (xc * dot(u4[pl.ds(r0, Q), :], e4[:, cols])).astype(BF16)
                ub[pl.ds(r0, Q), cols] = u
                fresh = dot(b_turned, u)
                pst[b, :, cols] = fresh
                scaled = rt[pl.ds(b, 1), cols] * fresh
                fac[:, cols] = jnp.where(turn == 0, scaled, fac[:, cols] + scaled)
            return carry

        lax.fori_loop(0, blocks, first_pass, 0)
        for rp in range(row_parts):
            for cp in range(g * col_parts // groups, (g + 1) * col_parts // groups):
                fmsg[rp * col_parts + cp] = fac[
                    rp * 16 : (rp + 1) * 16, cp * part : (cp + 1) * part
                ].astype(BF16)

        def send_state(k, carry, g=g):
            j = lax.rem(me + k, ns)

            @pl.when(lax.div(lax.rem(j, col_parts), col_parts // groups) == g)
            def _():
                to_seq(fmsg, frecv, f_s, f_r, j, me, j).start()

            return carry

        lax.fori_loop(1, ns, send_state, 0)

    def recur(tile, carry):
        cols = pl.ds(pl.multiple_of(tile * 128, 128), 128)
        state = jnp.zeros((N, 128), F32)
        for b in range(blocks):
            fresh = pst[b, :, cols]
            pst[b, :, cols] = state
            state = et[b : b + 1, cols] * (fresh + em[b : b + 1, cols] * state)
        return carry

    lax.fori_loop(0, width // 128, recur, 0)

    def await_decay(k, carry):
        j = lax.rem(me + k, ns)
        pltpu.make_async_remote_copy(
            src_ref=dl_all.at[j],
            dst_ref=dl_all.at[j],
            send_sem=dl_s.at[j],
            recv_sem=dl_r.at[j],
            device_id=(j, d),
            device_id_type=MESH,
        ).wait_recv()
        return carry

    lax.fori_loop(1, ns, await_decay, 0)
    mine = pl.multiple_of(lax.rem(me, col_parts) * part, part)
    dexp[...] = dot(
        pack(jnp.exp(dl_all[...].reshape(ns * 8, lanes))), e4[:, pl.ds(mine, part)]
    )
    frecv[me] = fmsg[me]

    def relay(i, state):
        @pl.when(i != me)
        def _():
            to_seq(fmsg, frecv, f_s, f_r, i, i, i).wait_recv()

        imsg[i] = state.astype(BF16)

        @pl.when(i != me)
        def _():
            to_seq(imsg, irecv, i_s, i_r, i, me, i).start()

        fade = dexp[pl.ds(pl.multiple_of(i * 8, 8), 8), :]
        return jnp.concatenate([fade, fade], 0) * state + frecv[i].astype(F32)

    lax.fori_loop(0, ns, relay, jnp.zeros((16, part), F32))
    irecv[me] = imsg[me]

    def await_state(k, carry):
        j = lax.rem(me + k, ns)
        to_seq(imsg, irecv, i_s, i_r, j, j, j).wait_recv()
        return carry

    lax.fori_loop(1, ns, await_state, 0)
    for rp in range(row_parts):
        for cp in range(col_parts):
            fac[rp * 16 : (rp + 1) * 16, cp * part : (cp + 1) * part] = irecv[
                rp * col_parts + cp
            ].astype(F32)
    load_z.wait()

    mask = lax.broadcasted_iota(jnp.int32, (Q, Q), 0) >= lax.broadcasted_iota(jnp.int32, (Q, Q), 1)

    def second_pass(chunk):
        def one(i, carry):
            b = chunk * (chunk_rows // Q) + i
            r0 = pl.multiple_of(b * Q, Q)
            for g in range(groups):
                b_mat = bcb[pl.ds(r0 + LEAD, Q), g * 2 * N : g * 2 * N + N]
                c_mat = bcb[pl.ds(r0 + LEAD, Q), g * 2 * N + N : (g + 1) * 2 * N]
                scores = lax.dot_general(
                    c_mat, b_mat, (((1,), (1,)), ((), ())), preferred_element_type=F32
                )
                lhs = jnp.concatenate([jnp.where(mask, scores, 0.0).astype(BF16), c_mat], 1)
                squares = jnp.zeros((Q, 128), F32)
                for tile in range(gw // TILE):
                    cols = slice(g * gw + tile * TILE, g * gw + (tile + 1) * TILE)
                    entering = em[pl.ds(b, 1), cols] * (
                        pst[b, :, cols] + eo[pl.ds(b, 1), cols] * fac[:, cols]
                    )
                    rhs = jnp.concatenate([ub[pl.ds(r0, Q), cols], entering.astype(BF16)], 0)
                    y = dot(a4[pl.ds(r0, Q), :], e4[:, cols]) * dot(lhs, rhs)
                    y = y + skx[0:1, cols] * xb[pl.ds(r0 + LEAD, Q), cols].astype(F32)
                    gated = y * silu(zb[pl.ds(r0, Q), cols].astype(F32))
                    gbuf[:, tile * TILE : (tile + 1) * TILE] = gated
                    for k in range(TILE // 128):
                        squares = squares + gated[:, k * 128 : (k + 1) * 128] ** 2
                mean = jnp.sum(squares, axis=1, keepdims=True) * (1.0 / gw)
                scale = lax.rsqrt(mean + EPS)
                for tile in range(gw // TILE):
                    cols = slice(g * gw + tile * TILE, g * gw + (tile + 1) * TILE)
                    ub[pl.ds(r0, Q), cols] = (
                        gbuf[:, tile * TILE : (tile + 1) * TILE] * scale * gain_ref[:, cols]
                    ).astype(BF16)
            return carry

        lax.fori_loop(0, chunk_rows // Q, one, 0)

    def product(way, p, chunk):
        first = pl.multiple_of(way * half + p * piece, piece)
        rows = pl.ds(pl.multiple_of(chunk * chunk_rows, chunk_rows), chunk_rows)
        return dot(ub[rows, :], wb[:, pl.ds(first, piece)])

    def hop(way, turn, p):
        return pltpu.make_async_remote_copy(
            src_ref=rs_send.at[way, turn, p],
            dst_ref=rs_recv.at[way, turn, p],
            send_sem=r_s.at[way, turn, p],
            recv_sem=r_r.at[way, turn, p],
            device_id=(me, jnp.where(way == 0, right, left)),
            device_id_type=MESH,
        )

    def stage(way, turn, p):
        chunk = lax.rem(jnp.where(way == 0, d + 2 * HEADS - 1 - turn, d + 1 + turn), HEADS)
        total = product(way, p, chunk)
        if turn > 0:
            hop(way, turn - 1, p).wait_recv()
            total = total + rs_recv[way, turn - 1, p].astype(F32)
        rs_send[way, turn, p] = total.astype(BF16)
        hop(way, turn, p).start()

    def first_stages(k, carry):
        second_pass(lax.rem(jnp.where(k == 0, left, right), HEADS))

        def run_piece(p, inner):
            stage(k, 0, p)
            return inner

        lax.fori_loop(0, PIECES, run_piece, 0)
        return carry

    def both(turn):
        def run_piece(q, carry):
            stage(lax.rem(q, 2), turn, lax.div(q, 2))
            return carry

        lax.fori_loop(0, 2 * PIECES, run_piece, 0)

    load_w(0).wait()
    load_w(1).wait()
    lax.fori_loop(0, 2, first_stages, 0)
    second_pass(lax.rem(d + 2, HEADS))
    both(1)
    second_pass(d)
    both(2)

    def own(q, carry):
        total = product(lax.rem(q, 2), lax.div(q, 2), d)
        pst[q, :, 0:piece] = total[:Q]
        pst[q, :, piece : 2 * piece] = total[Q:]
        return carry

    lax.fori_loop(0, 2 * PIECES, own, 0)

    def to_out(way, p):
        first = pl.multiple_of(way * half + p * piece, piece)
        return pltpu.make_async_copy(
            zb.at[
                pl.ds(pl.multiple_of(way * chunk_rows, chunk_rows), chunk_rows),
                pl.ds(pl.multiple_of(p * piece, piece), piece),
            ],
            out_hbm.at[:, pl.ds(first, piece)],
            out_sem.at[way, p],
        )

    def finish(q, carry):
        way, p = lax.rem(q, 2), lax.div(q, 2)
        hop(way, HEADS - 2, p).wait_recv()
        arrived = rs_recv[way, HEADS - 2, p].astype(F32)
        cols = pl.ds(pl.multiple_of(p * piece, piece), piece)
        base = pl.multiple_of(way * chunk_rows, chunk_rows)
        zb[pl.ds(base, Q), cols] = (pst[q, :, 0:piece] + arrived[:Q]).astype(BF16)
        zb[pl.ds(base + Q, Q), cols] = (pst[q, :, piece : 2 * piece] + arrived[Q:]).astype(BF16)
        to_out(way, p).start()
        return carry

    lax.fori_loop(0, 2 * PIECES, finish, 0)

    halo(0, x_hbm, xb).wait_send()
    halo(1, bc_hbm, bcb).wait_send()

    def await_sends(k, carry):
        j = lax.rem(me + k, ns)
        decay_copy(j).wait_send()
        to_seq(fmsg, frecv, f_s, f_r, j, me, j).wait_send()
        to_seq(imsg, irecv, i_s, i_r, j, me, j).wait_send()
        return carry

    lax.fori_loop(1, ns, await_sends, 0)

    def await_ring(q, carry):
        way, p = lax.rem(q, 2), lax.div(q, 2)
        for turn in range(HEADS - 1):
            hop(way, turn, p).wait_send()
        to_out(way, p).wait()
        return carry

    lax.fori_loop(0, 2 * PIECES, await_ring, 0)


def local(
    x_input,
    z_input,
    bc_input,
    conv_weight_x,
    conv_weight_bc,
    step_size,
    log_decay,
    skip_gain,
    norm_gain,
    out_weight,
):
    ns = lax.axis_size("seq")
    length, width = x_input.shape
    groups = bc_input.shape[1]
    columns = out_weight.shape[1]
    blocks = length // Q
    heads = step_size.shape[1]
    part = width // (ns // (N // 16))
    piece = columns // 2 // PIECES
    rows = length // HEADS
    any_space = pl.BlockSpec(memory_space=pl.ANY)
    vmem = pl.BlockSpec(memory_space=pltpu.VMEM)
    dma = pltpu.SemaphoreType.DMA
    return pl.pallas_call(
        functools.partial(kernel, ns),
        out_shape=jax.ShapeDtypeStruct((rows, columns), BF16),
        in_specs=[any_space] * 4 + [vmem] * 6,
        out_specs=any_space,
        scratch_shapes=[
            pltpu.VMEM((LEAD + length, width), BF16),
            pltpu.VMEM((length, width), BF16),
            pltpu.VMEM((LEAD + length, groups * 2 * N), BF16),
            pltpu.VMEM((width, columns), BF16),
            pltpu.VMEM((length, width), BF16),
            pltpu.VMEM((blocks, N, width), F32),
            pltpu.VMEM((N, width), F32),
            pltpu.VMEM((128, width), BF16),
            pltpu.VMEM((length, 128), BF16),
            pltpu.VMEM((length, 128), BF16),
            pltpu.VMEM((blocks, width), F32),
            pltpu.VMEM((blocks, width), F32),
            pltpu.VMEM((blocks, width), F32),
            pltpu.VMEM((blocks, width), F32),
            pltpu.VMEM((8, width), F32),
            pltpu.VMEM((ns, 8, 128), F32),
            pltpu.VMEM((ns * 8, part), F32),
            pltpu.VMEM((ns, 16, part), BF16),
            pltpu.VMEM((ns, 16, part), BF16),
            pltpu.VMEM((ns, 16, part), BF16),
            pltpu.VMEM((ns, 16, part), BF16),
            pltpu.VMEM((Q, width // groups), F32),
            pltpu.VMEM((2, HEADS - 1, PIECES, rows, piece), BF16),
            pltpu.VMEM((2, HEADS - 1, PIECES, rows, piece), BF16),
            dma((6,)),
            dma((2,)),
            dma((2,)),
            dma((ns,)),
            dma((ns,)),
            dma((ns,)),
            dma((ns,)),
            dma((ns,)),
            dma((ns,)),
            dma((2, HEADS - 1, PIECES)),
            dma((2, HEADS - 1, PIECES)),
            dma((2, PIECES)),
        ],
        compiler_params=pltpu.CompilerParams(
            collective_id=0, has_side_effects=True, vmem_limit_bytes=60 * 2**20
        ),
        cost_estimate=pl.CostEstimate(
            flops=2 * length * width * columns,
            bytes_accessed=2 * (2 * length * width + width * columns),
            transcendentals=2 * length * width,
        ),
    )(
        x_input,
        z_input,
        bc_input.reshape(length, groups * 2 * N),
        out_weight,
        conv_weight_x,
        conv_weight_bc.reshape(KCONV, groups * 2 * N),
        step_size,
        log_decay,
        skip_gain.reshape(1, heads),
        norm_gain.reshape(1, width),
    )


def solution(mesh):
    in_specs = (
        P("seq", "head"),
        P("seq", "head"),
        P("seq", "head", None),
        P(None, "head"),
        P(None, "head", None),
        P("seq", "head"),
        P("seq", "head"),
        P("head"),
        P("head"),
        P("head", None),
    )
    out_specs = P(("seq", "head"), None)
    return jax.shard_map(local, mesh=mesh, in_specs=in_specs, out_specs=out_specs, check_vma=False)
```

time: 961 us -> 128 us (0.13)
  waiting for transfers between devices: 564 us -> 0 us
  starting transfers between devices: 154 us -> 0 us
  Pallas kernels: 0 us -> 116 us
  matrix products: 82.6 us -> 0 us
  other arithmetic: 63.4 us -> 0 us
  local copies, waits for them, and re-layouts: 71.3 us -> 10.7 us
  between operations: 13.9 us -> 0.01 us
    ppermute x33 -> x0, waiting for transfers between devices: 363 us -> none  [from_behind(): return lax.ppermute(block, axis, route)]
    reduce_scatter x1 -> x0, waiting for transfers between devices: 201 us -> none  [local(): lax.psum_scatter(jnp.dot(normed, out_weight, preferred_element_type=jnp.f...]
    ppermute x33 -> x0, starting transfers between devices: 154 us -> none  [from_behind(): return lax.ppermute(block, axis, route)]
    pallas_call x0 -> x1, Pallas kernels: none -> 116 us  [local(): pl.pallas_call(functools.partial(kernel, ns), out_shape=jax.ShapeDtypeStr...]
    dot_general x5 -> x0, matrix products: 82.6 us -> none  [the longest x1 42 us: local(): jnp.einsum('ctsgh,csghp->ctghp', scores[..., None] * decay_table, driven,...]
    reshape x1 -> x0, other arithmetic: 17.2 us -> none  [local(): x_conv.astype(jnp.float32)]
    add x1 -> x0, local copies, waits for them, and re-layouts: 13.8 us -> none  [local(): within + carried + skip_gain.reshape(groups, per_group)[..., None] * x_float]
    add x35 -> x0, other arithmetic: 13.1 us -> none  [the longest x4 8.06 us: pass_block(): jnp.exp(log_total)[..., None, None] * carry_state + fresh]
  transfers between devices with their start and end apart: 34 -> 0, of which waited for: 32 -> 0; matrix products, arithmetic and copies ran while one was open for 4% -> 0% of each run, Pallas kernels for 0% -> 0%
where the time goes in v1:
time: 128 us; the launch traced here: 127 us
  Pallas kernels  116 us (91%)
  local copies, waits for them, and re-layouts  10.7 us (8%)
    pallas_call x1, Pallas kernels, local(): pl.pallas_call(functools.partial(kernel, ns), out_shape=jax.ShapeDtypeStr...  116 us
    unnamed x5, local copies, waits for them, and re-layouts  10.7 us

profile of v1, /device:TPU:1, one launch (start us, length us, event | category | flops | bytes accessed | tf_op | source)
XLA Modules:
  0.0 126.6 jit_solution(18382772883132921905)
XLA Ops:
  0.0 1.3 %copy.14 = f32[1,4,2,256]{3,1,2,0:T(4,128)} copy(f32[1,4,2,256]{3,2,1,0:T(2,128)} %bitcast.8) | data formatting | bytes 16384
  1.3 1.9 %copy.11.step_ref = f32[1024,32]{1,0:T(8,128)} copy(f32[1024,32]{0,1:T(8,128)} %param.15) | data formatting | bytes 262144 | tf_op args[5]
  3.2 1.9 %copy.12.ld_ref = f32[1024,32]{1,0:T(8,128)} copy(f32[1024,32]{0,1:T(8,128)} %param.16) | data formatting | bytes 262144 | tf_op args[6]
  5.1 2.4 %copy.13 = bf16[128,8,2,256]{3,1,2,0:T(8,128)(2,1)} copy(bf16[128,8,2,256]{3,2,1,0:T(2,128)(2,1)} %bitcast.6) | data formatting | bytes 2097152
  7.5 115.9 %shard_map.100 = bf16[256,4096]{1,0:T(8,128)(2,1)} custom-call(bf16[1024,2048]{1,0:T(8,128)(2,1)} %x_hbm.1, bf16[1024,2048]{1,0:T(8,128)(2,1)} %z_hbm.1, bf16[1024,512]{1,0:T(8,128)(2,1)} %bitcast.7, bf16[2048,4096]{1,0:T(8,128)(2,1)} %w_hbm.1, f32[4,2048]{1,0:T(4,128)} %cwx.1, f32[4,512]{1,0:T(4,128)} %bitcast.9, f32[1024,32]{1,0:T(8,128)} %copy.11.step_ref, ...), custom_call_target="tpu_custom_call" | custom-call | flops 17179869184 | bytes 25165824 | tf_op jit(solution)/shard_map/pallas_call | solution.py:535
  123.5 3.1 %copy.16 = bf16[256,4096]{1,0:T(8,128)(2,1)} copy(bf16[256,4096]{1,0:T(8,128)(2,1)} %shard_map.100) | data formatting | bytes 4194304

commit v2 on v1

v2 whole, which is shorter than its diff:
```python
import functools

import jax
import jax.numpy as jnp
from jax import lax
from jax.experimental import pallas as pl
from jax.experimental.pallas import tpu as pltpu
from jax.sharding import PartitionSpec as P

P_SIZE = 64
N = 128
KCONV = 4
EPS = 1e-05
Q = 128
LEAD = 16
TILE = 256
CONV_COLS = 256
PIECES = 4
HEADS = 4

MESH = pl.DeviceIdType.MESH
F32 = jnp.float32
BF16 = jnp.bfloat16


def split3(value):
    hi = value.astype(BF16)
    rest = value - hi.astype(F32)
    mid = rest.astype(BF16)
    return hi, mid, (rest - mid.astype(F32)).astype(BF16)


def dot(a, b):
    return jnp.dot(a, b, preferred_element_type=F32)


def kernel(
    ns,
    x_hbm,
    z_hbm,
    bc_hbm,
    w_hbm,
    cwx,
    cwbc,
    step_ref,
    ld_ref,
    skip_ref,
    gain_ref,
    out_hbm,
    xb,
    zb,
    bcr,
    bcb,
    wb,
    ub,
    pst,
    fac,
    e4,
    a4,
    u4,
    em,
    et,
    eo,
    rt,
    skx,
    taps_x,
    taps_bc,
    dl_pair,
    pair_send,
    pair_recv,
    fmsg,
    frecv,
    imsg,
    irecv,
    gbuf,
    rs_send,
    rs_recv,
    local_sem,
    halo_send,
    halo_recv,
    pair_s,
    pair_r,
    f_s,
    f_r,
    i_s,
    i_r,
    r_s,
    r_r,
    out_sem,
):
    length, width = x_hbm.shape
    columns = w_hbm.shape[1]
    heads = step_ref.shape[0]
    groups = bc_hbm.shape[1] // (2 * N)
    gw = width // groups
    blocks = length // Q
    chunk_rows = length // HEADS
    half = columns // 2
    piece = half // PIECES
    chips = ns // 2
    row_parts = N // 16
    col_parts = chips // row_parts
    part = gw // col_parts
    strip = LEAD + length
    strips = width // piece

    me = lax.axis_index("seq")
    d = lax.axis_index("head")
    right = lax.rem(d + 1, HEADS)
    left = lax.rem(d + HEADS - 1, HEADS)
    after = lax.rem(me + 1, ns)
    chip, core = lax.div(me, 2), lax.rem(me, 2)
    sibling = me + 1 - 2 * core

    barrier = pltpu.get_barrier_semaphore()

    def load_x(q):
        return pltpu.make_async_copy(
            x_hbm.at[:, pl.ds(pl.multiple_of(q * piece, piece), piece)],
            rs_send.at[pl.ds(pl.multiple_of(q * strip + LEAD, LEAD), length)],
            local_sem.at[q],
        )

    load_bc = pltpu.make_async_copy(bc_hbm, bcr.at[pl.ds(LEAD, length)], local_sem.at[strips])
    load_z = pltpu.make_async_copy(z_hbm, zb, local_sem.at[strips + 1])

    def load_w(h):
        return pltpu.make_async_copy(
            w_hbm.at[:, pl.ds(h * half, half)],
            wb.at[:, pl.ds(h * half, half)],
            local_sem.at[strips + 2 + h],
        )

    load_bc.start()
    per_group = strips // groups
    for q in range(per_group):
        load_x((1 - core) * per_group + q).start()
    for q in range(per_group):
        load_x(core * per_group + q).start()

    def greet(k, carry):
        other = 2 * lax.rem(chip + k, chips) + core
        pl.semaphore_signal(barrier, inc=1, device_id=(other, d), device_id_type=MESH)
        return carry

    lax.fori_loop(1, chips, greet, 0)
    across = lax.rem(jnp.where(core == 0, me + ns - 1, me + 1), ns)
    for other in (sibling, across):
        pl.semaphore_signal(barrier, inc=1, device_id=(other, d), device_id_type=MESH)
    for other in (right, left):
        pl.semaphore_signal(barrier, inc=1, device_id=(me, other), device_id_type=MESH)

    lanes = 128
    lane_row = lax.broadcasted_iota(jnp.int32, (lanes, TILE), 0)
    lane_col = lax.broadcasted_iota(jnp.int32, (lanes, TILE), 1)
    apart = jnp.where(
        lane_row < 3 * heads, lax.rem(lane_row, heads) - lax.div(lane_col, P_SIZE), -heads
    )
    for tile in range(width // TILE):
        e4[:, tile * TILE : (tile + 1) * TILE] = jnp.where(
            apart == tile * (TILE // P_SIZE), 1.0, 0.0
        ).astype(BF16)

    def pack(value):
        hi, mid, lo = split3(value)
        lane = lax.broadcasted_iota(jnp.int32, value.shape, 1)
        hi, mid, lo = hi.astype(F32), mid.astype(F32), lo.astype(F32)
        chosen = jnp.where(lane < heads, hi, jnp.where(lane < 2 * heads, mid, lo))
        return jnp.where(lane < 3 * heads, chosen, 0.0).astype(BF16)

    rep = jnp.where(
        lax.rem(lax.broadcasted_iota(jnp.int32, (heads, lanes), 1), heads)
        == lax.broadcasted_iota(jnp.int32, (heads, lanes), 0),
        1.0,
        0.0,
    ).astype(BF16)
    mask = lax.broadcasted_iota(jnp.int32, (Q, Q), 0) >= lax.broadcasted_iota(jnp.int32, (Q, Q), 1)
    low = jnp.where(mask, 1.0, 0.0).astype(BF16)

    def turned(parts, right_mat):
        total = 0.0
        for one in parts:
            total = total + lax.dot_general(
                one, right_mat, (((0,), (0,)), ((), ())), preferred_element_type=F32
            )
        return total

    def gap(b):
        return slice(b % 2 * Q, (b % 2 + 1) * Q), slice(b // 2 * lanes, (b // 2 + 1) * lanes)

    fades = slice(blocks // 2 * lanes, blocks // 2 * lanes + part)
    kept = slice(width - gw, width)

    mids, tots = [], []
    for b in range(blocks):
        rows = slice(b * Q, (b + 1) * Q)
        ld4 = turned(split3(ld_ref[:, rows]), rep)
        step4 = turned(split3(step_ref[:, rows]), rep)
        parts = split3(ld4)
        cum = dot(low, parts[0]) + dot(low, parts[1]) + dot(low, parts[2])
        mid = cum[Q // 2 - 1 : Q // 2, :]
        gbuf[gap(b)] = cum - mid
        u4[rows, :] = pack(step4 * jnp.exp(mid - cum))
        mids.append(mid)
        tots.append(cum[Q - 1 : Q, :])
    row = lax.broadcasted_iota(jnp.int32, (blocks, lanes), 0)
    zero = jnp.zeros((blocks, lanes), F32)
    m8, t8, o8, s8 = zero, zero, zero, zero
    run = jnp.zeros((1, lanes), F32)
    for b in range(blocks):
        m8 = jnp.where(row == b, mids[b], m8)
        t8 = jnp.where(row == b, tots[b], t8)
        o8 = jnp.where(row == b, run, o8)
        run = run + tots[b]
    dl_pair[0] = jnp.broadcast_to(run, (8, lanes))
    later = jnp.zeros((1, lanes), F32)
    for b in reversed(range(blocks)):
        s8 = jnp.where(row == b, later, s8)
        later = later + tots[b]
    rt[...] = dot(pack(jnp.exp(s8 + t8 - m8)), e4[...])
    fac[...] = jnp.zeros((N, width), F32)
    taps_x[...] = 0.5 * cwx[...]
    for k in range(KCONV):
        for g in range(groups):
            taps_bc[k : k + 1, g * 2 * N : (g + 1) * 2 * N] = 0.5 * cwbc[k, g : g + 1, :]

    def halo(q):
        src = bc_hbm.at[pl.ds(length - LEAD, LEAD)]
        dst = bcr.at[pl.ds(0, LEAD)]
        if q < strips:
            src = x_hbm.at[pl.ds(length - LEAD, LEAD), pl.ds(q * piece, piece)]
            dst = rs_send.at[pl.ds(q * strip, LEAD)]
        return pltpu.make_async_remote_copy(
            src_ref=src,
            dst_ref=dst,
            send_sem=halo_send.at[q],
            recv_sem=halo_recv.at[q],
            device_id=(after, d),
            device_id_type=MESH,
        )

    def to_seq(src, dst, send, recv, slot, there, other):
        return pltpu.make_async_remote_copy(
            src_ref=src.at[slot],
            dst_ref=dst.at[there],
            send_sem=send.at[0],
            recv_sem=recv.at[0],
            device_id=(other, d),
            device_id_type=MESH,
        )

    def all_of(ref, sem):
        others = ref.at[pl.ds(0, chips - 1)]
        return pltpu.make_async_copy(others, others, sem.at[0])

    def to_sibling(src, dst, slot):
        return pltpu.make_async_remote_copy(
            src_ref=src,
            dst_ref=dst,
            send_sem=pair_s.at[slot],
            recv_sem=pair_r.at[slot],
            device_id=(sibling, d),
            device_id_type=MESH,
        )

    def decays():
        return to_sibling(dl_pair.at[0], dl_pair.at[1], 2)

    def states(slot):
        return to_sibling(pair_send.at[slot], pair_recv.at[slot], slot)

    def conv(buf, taps, r0, cols, tap_cols):
        prev = buf[pl.ds(r0, LEAD), cols].astype(F32)[LEAD - 8 :]
        cur = buf[pl.ds(r0 + LEAD, Q), cols].astype(F32)
        ext = jnp.concatenate([prev, cur], 0)
        total = taps[KCONV - 1 : KCONV, tap_cols] * cur
        for k in range(1, KCONV):
            total = total + taps[KCONV - 1 - k : KCONV - k, tap_cols] * pltpu.roll(ext, k, 0)[8:]
        return total * jnp.tanh(total) + total

    def of_group(g, tile):
        return pl.ds(pl.multiple_of(g * gw + tile * TILE, TILE), TILE)

    def convolve(g, b):
        r0 = pl.multiple_of(b * Q, Q)
        both = pl.ds(pl.multiple_of(g * 2 * N, 2 * N), 2 * N)
        bcb[pl.ds(r0, Q), both] = conv(bcr, taps_bc, r0, both, both).astype(BF16)
        for k in range(gw // CONV_COLS):
            cols = pl.ds(pl.multiple_of(g * gw + k * CONV_COLS, CONV_COLS), CONV_COLS)
            inside = slice(k * CONV_COLS % piece, k * CONV_COLS % piece + CONV_COLS)
            q = g * per_group + k * CONV_COLS // piece
            xc = conv(rs_send, taps_x, pl.multiple_of(r0 + q * strip, LEAD), inside, cols).astype(BF16)
            xb[pl.ds(r0, Q), cols] = xc
            ub[pl.ds(r0, Q), cols] = (
                xc.astype(F32) * dot(u4[pl.ds(r0, Q), :], e4[:, cols])
            ).astype(BF16)

    def gather(g, b):
        r0 = pl.multiple_of(b * Q, Q)
        b_turned = bcb[pl.ds(r0, Q), pl.ds(pl.multiple_of(g * 2 * N, 2 * N), N)].astype(F32).T.astype(BF16)
        for tile in range(gw // TILE):
            cols = of_group(g, tile)
            fresh = dot(b_turned, ub[pl.ds(r0, Q), cols])
            pst[b, :, cols] = fresh
            fac[:, cols] = fac[:, cols] + rt[pl.ds(b, 1), cols] * fresh

    load_bc.wait()
    for q in range(strips):
        load_x(q).wait()
    load_z.start()
    load_w(0).start()
    load_w(1).start()

    def place(turn):
        early = turn < 2 * (blocks - 1)
        sent = (turn < blocks - 1) | (turn == 2 * (blocks - 1))
        return (
            jnp.where(sent, 1 - core, core),
            jnp.where(early, blocks - 1 - lax.rem(turn, blocks - 1), 0),
        )

    def first_pass(turn, carry):
        @pl.when(turn == blocks - 1)
        def _():
            pl.semaphore_wait(barrier, chips + 3)
            for q in range(strips + 1):
                halo(q).start()
            decays().start()

        @pl.when(turn == 2 * (blocks - 1))
        def _():
            for q in range(strips + 1):
                halo(q).wait_recv()

            @pl.when(me == 0)
            def _():
                for q in range(strips):
                    rs_send[q * strip : q * strip + LEAD, :] = jnp.zeros((LEAD, piece), BF16)
                bcr[:LEAD, :] = jnp.zeros((LEAD, bcr.shape[1]), BF16)

        gather(*place(turn - 1))
        convolve(*place(turn))

        @pl.when(turn == 2 * blocks - 1)
        def _():
            for tile in range(gw // TILE):
                pair_send[0, :, tile * TILE : (tile + 1) * TILE] = fac[
                    :, of_group(1 - core, tile)
                ].astype(BF16)
            states(0).start()

        return carry

    convolve(1 - core, blocks - 1)
    lax.fori_loop(1, 2 * blocks, first_pass, 0)
    gather(core, 0)

    decays().wait_recv()
    log_mine, log_other = dl_pair[0], dl_pair[1]
    first_core = core == 0
    of_core = pl.ds(pl.multiple_of(core * gw, gw), gw)
    fade_0 = dot(pack(jnp.exp(jnp.where(first_core, log_mine, log_other))), e4[:, of_core])
    fade_1 = dot(pack(jnp.exp(jnp.where(first_core, log_other, log_mine))), e4[:, of_core])
    fade_chip = pack(jnp.exp(log_mine + log_other)).astype(F32)
    fade_chip = jnp.concatenate([fade_chip, fade_chip], 0).astype(BF16)
    states(0).wait_recv()
    for rp in range(row_parts):
        for cp in range(col_parts):
            rows, cols = slice(rp * 16, (rp + 1) * 16), slice(cp * part, (cp + 1) * part)
            mine = fac[rows, pl.ds(pl.multiple_of(core * gw + cp * part, part), part)]
            other = pair_recv[0, rows, cols].astype(F32)
            state_0 = jnp.where(first_core, mine, other)
            state_1 = jnp.where(first_core, other, mine)
            faded = jnp.concatenate([fade_1[:, cols]] * 2, 0) * state_0
            gbuf[rows, width - gw + cp * part : width - gw + (cp + 1) * part] = state_0
            fmsg[rp * col_parts + cp, :, 0:part] = (faded + state_1).astype(BF16)
            fmsg[rp * col_parts + cp, :, part : part + lanes] = fade_chip

    def send_state(k, carry):
        j = lax.rem(chip + k, chips)
        to_seq(fmsg, frecv, f_s, f_r, j, chip, 2 * j + core).start()
        return carry

    lax.fori_loop(1, chips, send_state, 0)

    gbuf[N : N + 8, kept] = fade_0
    for ref, value in ((em, jnp.exp(m8)), (et, jnp.exp(t8 - m8)), (eo, jnp.exp(o8))):
        ref[...] = dot(pack(value), e4[...])
    parts = split3(jnp.broadcast_to(skip_ref[...], (8, heads)))
    skx[...] = dot(pack(dot(parts[0], rep) + dot(parts[1], rep) + dot(parts[2], rep)), e4[...])
    frecv_mine = fmsg[chip]
    for b in range(blocks):
        rows = slice(b * Q, (b + 1) * Q)
        a4[rows, :] = pack(jnp.exp(gbuf[gap(b)]))

    def recur(tile, carry):
        cols = pl.ds(pl.multiple_of(tile * 128, 128), 128)
        state = jnp.zeros((N, 128), F32)
        for b in range(blocks):
            fresh = pst[b, :, cols]
            pst[b, :, cols] = state
            state = et[b : b + 1, cols] * (fresh + em[b : b + 1, cols] * state)
        return carry

    lax.fori_loop(0, width // 128, recur, 0)

    all_of(frecv, f_r).wait()
    frecv[chip] = frecv_mine
    here = pl.multiple_of(core * gw + lax.rem(chip, col_parts) * part, part)
    arrived_fades = frecv[:, :, part : part + lanes].reshape(chips * 16, lanes)
    gbuf[: chips * 16, fades] = dot(arrived_fades, e4[:, pl.ds(here, part)])
    state = jnp.zeros((16, part), F32)
    for i in range(chips):
        imsg[i] = state.astype(BF16)
        state = gbuf[i * 16 : (i + 1) * 16, fades] * state + frecv[i, :, 0:part].astype(F32)

    def send_back(k, carry):
        j = lax.rem(chip + k, chips)
        to_seq(imsg, irecv, i_s, i_r, j, chip, 2 * j + core).start()
        return carry

    lax.fori_loop(1, chips, send_back, 0)
    irecv_mine = imsg[chip]
    all_of(irecv, i_r).wait()
    irecv[chip] = irecv_mine
    for rp in range(row_parts):
        for cp in range(col_parts):
            rows = slice(rp * 16, (rp + 1) * 16)
            cols = slice(width - gw + cp * part, width - gw + (cp + 1) * part)
            enters = irecv[rp * col_parts + cp].astype(F32)
            fade = gbuf[N : N + 8, cols]
            passed = jnp.concatenate([fade, fade], 0) * enters + gbuf[rows, cols]
            fac[rows, pl.ds(pl.multiple_of(core * gw + cp * part, part), part)] = jnp.where(
                first_core, enters, passed
            )
            pair_send[1, rows, cp * part : (cp + 1) * part] = jnp.where(
                first_core, passed, enters
            ).astype(BF16)
    states(1).start()
    load_z.wait()
    load_w(0).wait()
    load_w(1).wait()

    states(1).wait_recv()
    for tile in range(gw // TILE):
        fac[:, of_group(1 - core, tile)] = pair_recv[1, :, tile * TILE : (tile + 1) * TILE].astype(F32)

    def second_pass(chunk):
        for g in range(groups):
            for i in range(chunk_rows // Q):
                b = chunk * (chunk_rows // Q) + i
                r0 = pl.multiple_of(b * Q, Q)
                b_mat = bcb[pl.ds(r0, Q), slice(g * 2 * N, g * 2 * N + N)]
                c_mat = bcb[pl.ds(r0, Q), g * 2 * N + N : (g + 1) * 2 * N]
                scores = lax.dot_general(
                    c_mat, b_mat, (((1,), (1,)), ((), ())), preferred_element_type=F32
                )
                lhs = jnp.concatenate([jnp.where(mask, scores, 0.0).astype(BF16), c_mat], 1)
                for tile in range(gw // TILE):
                    cols = slice(g * gw + tile * TILE, g * gw + (tile + 1) * TILE)
                    entering = em[pl.ds(b, 1), cols] * (
                        pst[b, :, cols] + eo[pl.ds(b, 1), cols] * fac[:, cols]
                    )
                    rhs = jnp.concatenate([ub[pl.ds(r0, Q), cols], entering.astype(BF16)], 0)
                    y = dot(a4[pl.ds(r0, Q), :], e4[:, cols]) * dot(lhs, rhs)
                    y = y + skx[0:1, cols] * xb[pl.ds(r0, Q), cols].astype(F32)
                    z_half = 0.5 * zb[pl.ds(r0, Q), cols].astype(F32)
                    gbuf[i * Q : (i + 1) * Q, cols] = y * (z_half * jnp.tanh(z_half) + z_half)
        for i in range(chunk_rows // Q):
            r0 = pl.multiple_of((chunk * (chunk_rows // Q) + i) * Q, Q)
            for g in range(groups):
                squares = jnp.zeros((Q, 128), F32)
                for k in range(gw // 128):
                    gated = gbuf[i * Q : (i + 1) * Q, g * gw + k * 128 : g * gw + (k + 1) * 128]
                    squares = squares + gated * gated
                mean = jnp.sum(squares, axis=1, keepdims=True) * (1.0 / gw)
                scale = lax.rsqrt(mean + EPS)
                for tile in range(gw // TILE):
                    cols = slice(g * gw + tile * TILE, g * gw + (tile + 1) * TILE)
                    ub[pl.ds(r0, Q), cols] = (
                        gbuf[i * Q : (i + 1) * Q, cols] * scale * gain_ref[:, cols]
                    ).astype(BF16)

    def product(way, p, chunk):
        first = pl.multiple_of(way * half + p * piece, piece)
        rows = pl.ds(pl.multiple_of(chunk * chunk_rows, chunk_rows), chunk_rows)
        return dot(ub[rows, :], wb[:, pl.ds(first, piece)])

    def outgoing(way, turn, p):
        index = (lax.rem(turn, 2) * 2 + way) * PIECES + p
        return pl.ds(pl.multiple_of(index * chunk_rows, chunk_rows), chunk_rows)

    def hop(way, turn, p):
        return pltpu.make_async_remote_copy(
            src_ref=rs_send.at[outgoing(way, turn, p)],
            dst_ref=rs_recv.at[way, turn, p],
            send_sem=r_s.at[way, turn, p],
            recv_sem=r_r.at[way, turn, p],
            device_id=(me, jnp.where(way == 0, right, left)),
            device_id_type=MESH,
        )

    def stage(way, turn, p):
        chunk = lax.rem(jnp.where(way == 0, d + 2 * HEADS - 1 - turn, d + 1 + turn), HEADS)
        total = product(way, p, chunk)
        if not (isinstance(turn, int) and turn == 0):

            @pl.when(turn == 2)
            def _():
                hop(way, 0, p).wait_send()

            hop(way, turn - 1, p).wait_recv()
            total = total + rs_recv[way, turn - 1, p].astype(F32)
        rs_send[outgoing(way, turn, p), :] = total.astype(BF16)
        hop(way, turn, p).start()

    def first_stages(k, carry):
        @pl.when(k < 2)
        def _():
            second_pass(jnp.where(k == 0, left, right))

        stage(lax.rem(k, 2), 0, lax.div(k, 2))
        return carry

    lax.fori_loop(0, 2 * PIECES, first_stages, 0)

    def later_stages(k, carry):
        turn = 1 + lax.div(k, 2 * PIECES)
        q = lax.rem(k, 2 * PIECES)

        @pl.when(q == 0)
        def _():
            second_pass(lax.rem(jnp.where(turn == 1, d + 2, d), HEADS))

        stage(lax.rem(q, 2), turn, lax.div(q, 2))
        return carry

    lax.fori_loop(0, (HEADS - 2) * 2 * PIECES, later_stages, 0)

    def own(q, carry):
        total = product(lax.rem(q, 2), lax.div(q, 2), d)
        pst[q, :, 0:piece] = total[:Q]
        pst[q, :, piece : 2 * piece] = total[Q:]
        return carry

    lax.fori_loop(0, 2 * PIECES, own, 0)

    def to_out(way, p):
        first = pl.multiple_of(way * half + p * piece, piece)
        return pltpu.make_async_copy(
            zb.at[
                pl.ds(pl.multiple_of(way * chunk_rows, chunk_rows), chunk_rows),
                pl.ds(pl.multiple_of(p * piece, piece), piece),
            ],
            out_hbm.at[:, pl.ds(first, piece)],
            out_sem.at[way, p],
        )

    def finish(q, carry):
        way, p = lax.rem(q, 2), lax.div(q, 2)
        hop(way, HEADS - 2, p).wait_recv()
        arrived = rs_recv[way, HEADS - 2, p].astype(F32)
        cols = pl.ds(pl.multiple_of(p * piece, piece), piece)
        base = pl.multiple_of(way * chunk_rows, chunk_rows)
        zb[pl.ds(base, Q), cols] = (pst[q, :, 0:piece] + arrived[:Q]).astype(BF16)
        zb[pl.ds(base + Q, Q), cols] = (pst[q, :, piece : 2 * piece] + arrived[Q:]).astype(BF16)
        to_out(way, p).start()
        return carry

    lax.fori_loop(0, 2 * PIECES, finish, 0)

    for q in range(strips + 1):
        halo(q).wait_send()
    decays().wait_send()
    states(0).wait_send()
    states(1).wait_send()
    all_of(fmsg, f_s).wait()
    all_of(imsg, i_s).wait()

    def await_ring(q, carry):
        way, p = lax.rem(q, 2), lax.div(q, 2)
        for turn in range(1, HEADS - 1):
            hop(way, turn, p).wait_send()
        to_out(way, p).wait()
        return carry

    lax.fori_loop(0, 2 * PIECES, await_ring, 0)


def local(
    x_input,
    z_input,
    bc_input,
    conv_weight_x,
    conv_weight_bc,
    step_size,
    log_decay,
    skip_gain,
    norm_gain,
    out_weight,
):
    ns = lax.axis_size("seq")
    length, width = x_input.shape
    groups = bc_input.shape[1]
    columns = out_weight.shape[1]
    blocks = length // Q
    heads = step_size.shape[1]
    chips = ns // 2
    part = width // groups // (chips // (N // 16))
    piece = columns // 2 // PIECES
    rows = length // HEADS
    any_space = pl.BlockSpec(memory_space=pl.ANY)
    vmem = pl.BlockSpec(memory_space=pltpu.VMEM)
    dma = pltpu.SemaphoreType.DMA
    return pl.pallas_call(
        functools.partial(kernel, ns),
        out_shape=jax.ShapeDtypeStruct((rows, columns), BF16),
        in_specs=[any_space] * 4 + [vmem] * 6,
        out_specs=any_space,
        scratch_shapes=[
            pltpu.VMEM((length, width), BF16),
            pltpu.VMEM((length, width), BF16),
            pltpu.VMEM((LEAD + length, groups * 2 * N), BF16),
            pltpu.VMEM((length, groups * 2 * N), BF16),
            pltpu.VMEM((width, columns), BF16),
            pltpu.VMEM((length, width), BF16),
            pltpu.VMEM((blocks, N, width), F32),
            pltpu.VMEM((N, width), F32),
            pltpu.VMEM((128, width), BF16),
            pltpu.VMEM((length, 128), BF16),
            pltpu.VMEM((length, 128), BF16),
            pltpu.VMEM((blocks, width), F32),
            pltpu.VMEM((blocks, width), F32),
            pltpu.VMEM((blocks, width), F32),
            pltpu.VMEM((blocks, width), F32),
            pltpu.VMEM((8, width), F32),
            pltpu.VMEM((KCONV, width), F32),
            pltpu.VMEM((KCONV, groups * 2 * N), F32),
            pltpu.VMEM((2, 8, 128), F32),
            pltpu.VMEM((2, N, width // groups), BF16),
            pltpu.VMEM((2, N, width // groups), BF16),
            pltpu.VMEM((chips, 16, part + 128), BF16),
            pltpu.VMEM((chips, 16, part + 128), BF16),
            pltpu.VMEM((chips, 16, part), BF16),
            pltpu.VMEM((chips, 16, part), BF16),
            pltpu.VMEM((rows, width), F32),
            pltpu.VMEM((max(4 * PIECES * rows, width // piece * (LEAD + length)), piece), BF16),
            pltpu.VMEM((2, HEADS - 1, PIECES, rows, piece), BF16),
            dma((width // piece + 4,)),
            dma((width // piece + 1,)),
            dma((width // piece + 1,)),
            dma((3,)),
            dma((3,)),
            dma((1,)),
            dma((1,)),
            dma((1,)),
            dma((1,)),
            dma((2, HEADS - 1, PIECES)),
            dma((2, HEADS - 1, PIECES)),
            dma((2, PIECES)),
        ],
        compiler_params=pltpu.CompilerParams(
            collective_id=0, has_side_effects=True, vmem_limit_bytes=60 * 2**20
        ),
        cost_estimate=pl.CostEstimate(
            flops=2 * length * width * columns,
            bytes_accessed=2 * (2 * length * width + width * columns),
            transcendentals=2 * length * width,
        ),
    )(
        x_input,
        z_input,
        bc_input.reshape(length, groups * 2 * N),
        out_weight,
        conv_weight_x,
        conv_weight_bc,
        step_size.T,
        log_decay.T,
        skip_gain.reshape(1, heads),
        norm_gain.reshape(1, width),
    )


def solution(mesh):
    in_specs = (
        P("seq", "head"),
        P("seq", "head"),
        P("seq", "head", None),
        P(None, "head"),
        P(None, "head", None),
        P("seq", "head"),
        P("seq", "head"),
        P("head"),
        P("head"),
        P("head", None),
    )
    out_specs = P(("seq", "head"), None)
    return jax.shard_map(local, mesh=mesh, in_specs=in_specs, out_specs=out_specs, check_vma=False)
```

time: 128 us -> 117 us (0.914)
  local copies, waits for them, and re-layouts: 10.7 us -> 5.55 us
  Pallas kernels: 116 us -> 111 us
    unnamed x5 -> x2, local copies, waits for them, and re-layouts: 10.7 us -> 5.55 us
    pallas_call x1, Pallas kernels: 116 us -> 111 us  [local(): pl.pallas_call(functools.partial(kernel, ns), out_shape=jax.ShapeDtypeStr...]
where the time goes in v2:
time: 117 us
  Pallas kernels  111 us (95%)
  local copies, waits for them, and re-layouts  5.55 us (5%)
    pallas_call x1, Pallas kernels, local(): pl.pallas_call(functools.partial(kernel, ns), out_shape=jax.ShapeDtypeStr...  111 us
    unnamed x2, local copies, waits for them, and re-layouts  5.55 us

profile of v2, /device:TPU:1, one launch (start us, length us, event | category | flops | bytes accessed | tf_op | source)
XLA Modules:
  0.0 116.5 jit_solution(18157535205107101443)
XLA Ops:
  0.0 2.4 %copy.11 = bf16[128,8,2,256]{3,1,2,0:T(8,128)(2,1)} copy(bf16[128,8,2,256]{3,2,1,0:T(2,128)(2,1)} %bitcast.6) | data formatting | bytes 2097152
  2.4 110.9 %shard_map.100 = bf16[256,4096]{1,0:T(8,128)(2,1)} custom-call(bf16[1024,2048]{1,0:T(8,128)(2,1)} %x_hbm.1, bf16[1024,2048]{1,0:T(8,128)(2,1)} %z_hbm.1, bf16[1024,512]{1,0:T(8,128)(2,1)} %bitcast.7, bf16[2048,4096]{1,0:T(8,128)(2,1)} %w_hbm.1, f32[4,2048]{1,0:T(4,128)} %cwx.1, f32[4,2,256]{2,1,0:T(2,128)} %cwbc.1, f32[32,1024]{1,0:T(8,128)} %bitcast.8, ...), custom_call_target="tpu_custom_call" | custom-call | flops 17179869184 | bytes 25165824 | tf_op jit(solution)/shard_map/pallas_call | solution.py:615
  113.4 3.1 %copy.13 = bf16[256,4096]{1,0:T(8,128)(2,1)} copy(bf16[256,4096]{1,0:T(8,128)(2,1)} %shard_map.100) | data formatting | bytes 4194304

commit v3 on v2

--- a/solution.py
+++ b/solution.py
@@ -305,29 +305,36 @@
             fac[:, cols] = fac[:, cols] + rt[pl.ds(b, 1), cols] * fresh
 
     load_bc.wait()
-    for q in range(strips):
-        load_x(q).wait()
-    load_z.start()
-    load_w(0).start()
-    load_w(1).start()
+    for q in range(per_group):
+        load_x((1 - core) * per_group + q).wait()
+
+    lead_turn = blocks + blocks // 2 - 1
 
     def place(turn):
-        early = turn < 2 * (blocks - 1)
-        sent = (turn < blocks - 1) | (turn == 2 * (blocks - 1))
+        sent = (turn < blocks - 1) | (turn == lead_turn)
+        others = jnp.where(turn < lead_turn, 2 * blocks - 2 - turn, 2 * blocks - 1 - turn)
         return (
             jnp.where(sent, 1 - core, core),
-            jnp.where(early, blocks - 1 - lax.rem(turn, blocks - 1), 0),
+            jnp.where(turn < blocks - 1, blocks - 1 - turn, jnp.where(turn == lead_turn, 0, others)),
         )
 
     def first_pass(turn, carry):
         @pl.when(turn == blocks - 1)
+        def _():
+            for q in range(per_group):
+                load_x(core * per_group + q).wait()
+            load_z.start()
+            load_w(0).start()
+            load_w(1).start()
+
+        @pl.when(turn == blocks - 3)
         def _():
             pl.semaphore_wait(barrier, chips + 3)
             for q in range(strips + 1):
                 halo(q).start()
             decays().start()
 
-        @pl.when(turn == 2 * (blocks - 1))
+        @pl.when(turn == lead_turn)
         def _():
             for q in range(strips + 1):
                 halo(q).wait_recv()
@@ -341,7 +348,7 @@
         gather(*place(turn - 1))
         convolve(*place(turn))
 
-        @pl.when(turn == 2 * blocks - 1)
+        @pl.when(turn == lead_turn + 1)
         def _():
             for tile in range(gw // TILE):
                 pair_send[0, :, tile * TILE : (tile + 1) * TILE] = fac[
@@ -381,7 +388,7 @@
         to_seq(fmsg, frecv, f_s, f_r, j, chip, 2 * j + core).start()
         return carry
 
-    lax.fori_loop(1, chips, send_state, 0)
+    lax.fori_loop(1, chips, send_state, 0, unroll=True)
 
     gbuf[N : N + 8, kept] = fade_0
     for ref, value in ((em, jnp.exp(m8)), (et, jnp.exp(t8 - m8)), (eo, jnp.exp(o8))):
@@ -419,7 +426,7 @@
         to_seq(imsg, irecv, i_s, i_r, j, chip, 2 * j + core).start()
         return carry
 
-    lax.fori_loop(1, chips, send_back, 0)
+    lax.fori_loop(1, chips, send_back, 0, unroll=True)
     irecv_mine = imsg[chip]
     all_of(irecv, i_r).wait()
     irecv[chip] = irecv_mine

time: 117 us -> 114 us (0.974)
  Pallas kernels: 111 us -> 109 us
    pallas_call x1, Pallas kernels: 111 us -> 109 us  [local(): pl.pallas_call(functools.partial(kernel, ns), out_shape=jax.ShapeDtypeStr...]
where the time goes in v3:
time: 114 us
  Pallas kernels  109 us (96%)
  local copies, waits for them, and re-layouts  5.55 us (5%)
    pallas_call x1, Pallas kernels, local(): pl.pallas_call(functools.partial(kernel, ns), out_shape=jax.ShapeDtypeStr...  109 us
    unnamed x2, local copies, waits for them, and re-layouts  5.55 us

profile of v3, /device:TPU:1, one launch (start us, length us, event | category | flops | bytes accessed | tf_op | source)
XLA Modules:
  0.0 114.3 jit_solution(866826700363421810)
XLA Ops:
  0.0 2.4 %copy.11 = bf16[128,8,2,256]{3,1,2,0:T(8,128)(2,1)} copy(bf16[128,8,2,256]{3,2,1,0:T(2,128)(2,1)} %bitcast.6) | data formatting | bytes 2097152
  2.4 108.8 %shard_map.100 = bf16[256,4096]{1,0:T(8,128)(2,1)} custom-call(bf16[1024,2048]{1,0:T(8,128)(2,1)} %x_hbm.1, bf16[1024,2048]{1,0:T(8,128)(2,1)} %z_hbm.1, bf16[1024,512]{1,0:T(8,128)(2,1)} %bitcast.7, bf16[2048,4096]{1,0:T(8,128)(2,1)} %w_hbm.1, f32[4,2048]{1,0:T(4,128)} %cwx.1, f32[4,2,256]{2,1,0:T(2,128)} %cwbc.1, f32[32,1024]{1,0:T(8,128)} %bitcast.8, ...), custom_call_target="tpu_custom_call" | custom-call | flops 17179869184 | bytes 25165824 | tf_op jit(solution)/shard_map/pallas_call | solution.py:622
  111.2 3.1 %copy.13 = bf16[256,4096]{1,0:T(8,128)(2,1)} copy(bf16[256,4096]{1,0:T(8,128)(2,1)} %shard_map.100) | data formatting | bytes 4194304

commit v4 on v3

--- a/solution.py
+++ b/solution.py
@@ -269,6 +269,10 @@
     def states(slot):
         return to_sibling(pair_send.at[slot], pair_recv.at[slot], slot)
 
+    def back(cp):
+        cols = pl.ds(cp * part, part)
+        return to_sibling(pair_send.at[1, :, cols], pair_recv.at[1, :, cols], 1 if cp == 0 else 2 + cp)
+
     def conv(buf, taps, r0, cols, tap_cols):
         prev = buf[pl.ds(r0, LEAD), cols].astype(F32)[LEAD - 8 :]
         cur = buf[pl.ds(r0 + LEAD, Q), cols].astype(F32)
@@ -430,8 +434,8 @@
     irecv_mine = imsg[chip]
     all_of(irecv, i_r).wait()
     irecv[chip] = irecv_mine
-    for rp in range(row_parts):
-        for cp in range(col_parts):
+    for cp in range(col_parts):
+        for rp in range(row_parts):
             rows = slice(rp * 16, (rp + 1) * 16)
             cols = slice(width - gw + cp * part, width - gw + (cp + 1) * part)
             enters = irecv[rp * col_parts + cp].astype(F32)
@@ -443,14 +447,15 @@
             pair_send[1, rows, cp * part : (cp + 1) * part] = jnp.where(
                 first_core, passed, enters
             ).astype(BF16)
-    states(1).start()
+        back(cp).start()
     load_z.wait()
     load_w(0).wait()
     load_w(1).wait()
 
-    states(1).wait_recv()
-    for tile in range(gw // TILE):
-        fac[:, of_group(1 - core, tile)] = pair_recv[1, :, tile * TILE : (tile + 1) * TILE].astype(F32)
+    for cp in range(col_parts):
+        back(cp).wait_recv()
+        for tile in range(cp * part // TILE, (cp + 1) * part // TILE):
+            fac[:, of_group(1 - core, tile)] = pair_recv[1, :, tile * TILE : (tile + 1) * TILE].astype(F32)
 
     def second_pass(chunk):
         for g in range(groups):
@@ -580,7 +585,8 @@
         halo(q).wait_send()
     decays().wait_send()
     states(0).wait_send()
-    states(1).wait_send()
+    for cp in range(col_parts):
+        back(cp).wait_send()
     all_of(fmsg, f_s).wait()
     all_of(imsg, i_s).wait()
 
@@ -656,8 +662,8 @@
             dma((width // piece + 4,)),
             dma((width // piece + 1,)),
             dma((width // piece + 1,)),
-            dma((3,)),
-            dma((3,)),
+            dma((2 + chips // (N // 16),)),
+            dma((2 + chips // (N // 16),)),
             dma((1,)),
             dma((1,)),
             dma((1,)),

time: 114 us -> 115 us (level)
  no operation moved by 1% of the time
where the time goes in v4:
time: 115 us; the launch traced here: 114 us
  Pallas kernels  109 us (95%)
  local copies, waits for them, and re-layouts  5.55 us (5%)
    pallas_call x1, Pallas kernels, local(): pl.pallas_call(functools.partial(kernel, ns), out_shape=jax.ShapeDtypeStr...  109 us
    unnamed x2, local copies, waits for them, and re-layouts  5.55 us

profile of v4, /device:TPU:1, one launch (start us, length us, event | category | flops | bytes accessed | tf_op | source)
XLA Modules:
  0.0 114.3 jit_solution(7994123034415415623)
XLA Ops:
  0.0 2.4 %copy.11 = bf16[128,8,2,256]{3,1,2,0:T(8,128)(2,1)} copy(bf16[128,8,2,256]{3,2,1,0:T(2,128)(2,1)} %bitcast.6) | data formatting | bytes 2097152
  2.4 108.8 %shard_map.100 = bf16[256,4096]{1,0:T(8,128)(2,1)} custom-call(bf16[1024,2048]{1,0:T(8,128)(2,1)} %x_hbm.1, bf16[1024,2048]{1,0:T(8,128)(2,1)} %z_hbm.1, bf16[1024,512]{1,0:T(8,128)(2,1)} %bitcast.7, bf16[2048,4096]{1,0:T(8,128)(2,1)} %w_hbm.1, f32[4,2048]{1,0:T(4,128)} %cwx.1, f32[4,2,256]{2,1,0:T(2,128)} %cwbc.1, f32[32,1024]{1,0:T(8,128)} %bitcast.8, ...), custom_call_target="tpu_custom_call" | custom-call | flops 17179869184 | bytes 25165824 | tf_op jit(solution)/shard_map/pallas_call | solution.py:628
  111.2 3.1 %copy.13 = bf16[256,4096]{1,0:T(8,128)(2,1)} copy(bf16[256,4096]{1,0:T(8,128)(2,1)} %shard_map.100) | data formatting | bytes 4194304
